TPU v7x, 32 devices: a whole 2x2x4 slice. The times are simulated.
32 devices in a mesh: row: 4 (over z), col: 8 (over y, x, core).
Axes of the slice: x: 2, y: 2, z: 4, core: 2. Of those that a mesh axis runs over, the one named last changes fastest.
Arguments:
- coeffs: float32 [512, 3, 64, 128], P(('row', 'col')), may hold values from -0.18 to 0.18
- degree: int32 [512], P(('row', 'col')), may hold values from 16 to 63
- material: float32 [512, 2], P(('row', 'col')), may hold values from 0.2 to 2
- split_coeffs: float32 [128, 3, 64, 64], P(('row', 'col')), may hold values from -0.18 to 0.18
- split_material: float32 [64, 2], replicated, may hold values from 0.2 to 2
- separation: float32 [3, 512, 8], P(None, ('row', 'col')), may hold values from -2.6 to 2.6, as said below
- reader_dev: int32 [512, 8], P(('row', 'col')), may hold values from 0 to 31, all different within a row; in each aligned block of 16 rows (0 to 15, 16 to 31, ...) at most 6 rows name the same one
- reader_slot: int32 [512, 8], P(('row', 'col')), may hold values from 0 to 15
Outputs:
- traction_coeffs: float32 [512, 64, 128], P(('row', 'col'))
- split_traction: float32 [128, 64, 64], P(('row', 'col'))
- near_velocity: float32 [3, 2048], P(None, ('row', 'col'))
Inputs may be any that keep to these rules, and one draw needn't show every extreme that they name: `reader_dev`: each ordinary drop names 8 different devices; among the drops of one device at most 6 name the same device, and some device is named exactly 6 times. Each entry's separation vector has a length between 1.9 and 2.6.
All inputs are finite; a program needn't handle non-finite values.
Results may differ from a plain program's by a relative error of at most 0.019.
Values may be sent and summed in bfloat16 or wider, within the bound.
A program may use at most 128 MiB of HBM per device.

v0:
```python
import math

import jax
import jax.numpy as jnp
import numpy as np
from jax import lax
from jax.sharding import PartitionSpec as P

HIGH = lax.Precision.HIGHEST
SOFTENING = 0.04


def from_partner(block, axis, stride):
    count = lax.axis_size(axis)
    route = []
    for low in range(count):
        high = low | 1 << stride
        if high != low and high < count:
            route += [(low, high), (high, low)]
    return lax.ppermute(block, axis, route)


def spectral_tables(degrees):
    nlon = 2 * degrees
    theta_lat = (np.arange(degrees) + 0.5) * (math.pi / degrees)
    cosine = np.cos(theta_lat)
    sine_theta = np.sin(theta_lat)
    legendre = np.zeros((degrees, degrees, degrees))
    for order in range(degrees):
        log_total = 0.0
        for step_index in range(1, order + 1):
            log_total = log_total + math.log((2.0 * step_index + 1.0) / (2.0 * step_index))
        diag_value = np.exp(0.5 * log_total + order * np.log(sine_theta)) / math.sqrt(4.0 * math.pi)
        legendre[order, :, order] = diag_value
        prev_two = diag_value
        if order + 1 < degrees:
            prev_one = math.sqrt(2.0 * order + 3.0) * cosine * diag_value
            legendre[order, :, order + 1] = prev_one
            for level in range(order + 2, degrees):
                alpha_term = math.sqrt(
                    (4.0 * level * level - 1.0) / (level * level - order * order)
                )
                beta_term = math.sqrt(
                    ((level - 1.0) ** 2 - order * order) / (4.0 * (level - 1.0) ** 2 - 1.0)
                )
                current = alpha_term * (cosine * prev_one - beta_term * prev_two)
                legendre[order, :, level] = current
                prev_two = prev_one
                prev_one = current
    order_index = np.arange(degrees)
    lon_index = np.arange(nlon)
    phase_angle = order_index[:, None] * lon_index[None, :] % nlon * (2.0 * math.pi / nlon)
    fourier = np.concatenate([np.cos(phase_angle), np.sin(phase_angle)], axis=0)
    quad_weight = sine_theta * (math.pi / degrees) * (2.0 * math.pi / nlon)
    longitude = lon_index * (2.0 * math.pi / nlon)
    normals = np.stack(
        [
            sine_theta[:, None] * np.cos(longitude)[None, :],
            sine_theta[:, None] * np.sin(longitude)[None, :],
            cosine[:, None] * np.ones((1, nlon)),
        ],
        axis=0,
    )
    return (
        jnp.asarray(legendre, dtype=jnp.float32),
        jnp.asarray(fourier, dtype=jnp.float32),
        jnp.asarray(quad_weight, dtype=jnp.float32),
        jnp.asarray(normals, dtype=jnp.float32),
    )


def legendre_synth(coeff, legendre):
    batch_size, degrees, coef_width = coeff.shape
    orders = legendre.shape[0]
    parted = coeff.reshape(batch_size, degrees, 2, orders)
    return jnp.einsum("mjl,nlcm->njcm", legendre, parted, precision=HIGH)


def fourier_synth(partial_legendre, fourier_rows):
    batch_size, nlat, two, orders = partial_legendre.shape
    return jnp.einsum(
        "njw,wk->njk",
        partial_legendre.reshape(batch_size, nlat, two * orders),
        fourier_rows,
        precision=HIGH,
    )


def analysis_fourier(traction_grid, fourier, quad_weight):
    batch_size, nlat, nlon = traction_grid.shape
    projected = (
        jnp.einsum("bjk,wk->bjw", traction_grid, fourier, precision=HIGH)
        * quad_weight[None, :, None]
    )
    return projected.reshape(batch_size, nlat, 2, fourier.shape[0] // 2)


def analysis_legendre(coef_grid, legendre):
    batch_size = coef_grid.shape[0]
    result = jnp.einsum("mjl,bjcm->blcm", legendre, coef_grid, precision=HIGH)
    return result.reshape(batch_size, legendre.shape[2], 2 * legendre.shape[0])


def prepare(coeffs, keep_mask):
    degrees = coeffs.shape[2]
    degree_value = jnp.arange(degrees, dtype=jnp.float32)
    shape_part = coeffs[:, 0] * keep_mask
    curvature = (
        shape_part * (degree_value * (degree_value + 1.0) / (degrees * degrees))[None, :, None]
    )
    electric = 3.0 * coeffs[:, 1] * keep_mask
    viscous = 3.0 * coeffs[:, 2] * keep_mask * ((degree_value + 2.0) / degrees)[None, :, None]
    return jnp.stack([shape_part, curvature, electric, viscous], axis=1)


def traction(surface, material):
    radius = jnp.exp(surface[:, 0])
    traction_grid = (
        material[:, 0, None, None] * surface[:, 1]
        + 0.5 * surface[:, 2] * surface[:, 2]
        + 2.0 * material[:, 1, None, None] * surface[:, 3]
    )
    return (radius, traction_grid)


def velocity_terms(
    radius, traction_grid, spacing, target_radius, cell_weight, cell_normal, target_normal
):
    load_grid = traction_grid * radius * radius * cell_weight[None, :]
    target_point = spacing[:, :, None] + target_radius[None] * target_normal[:, None, :]
    surface_point = radius[None] * cell_normal[:, None, :]
    offset = target_point[:, :, :, None] - surface_point[:, :, None, :]
    distance_sq = jnp.sum(offset * offset, axis=0)
    softened = distance_sq + SOFTENING
    weight = load_grid[:, None, :] / (softened * jnp.sqrt(softened))
    normal_dot = jnp.sum(offset * cell_normal[:, None, None, :], axis=0)
    stokeslet = weight[None] * (
        cell_normal[:, None, None, :] * (distance_sq + 2.0 * SOFTENING)[None]
        + offset * normal_dot[None]
    )
    return jnp.sum(stokeslet, axis=3) / (8.0 * math.pi)


def per_device(
    coeffs, degree, material, split_coeffs, split_material, separation, reader_dev, reader_slot
):
    drop_count, fields, degrees, coef_width = coeffs.shape
    legendre, fourier, quad_weight, normals = spectral_tables(degrees)
    nlat = legendre.shape[1]
    nlon = fourier.shape[1]
    degree_index = jnp.arange(degrees, dtype=jnp.int32)
    order_full = jnp.arange(coef_width, dtype=jnp.int32) % degrees
    order_mask = (degree_index[:, None] >= order_full[None, :]).astype(jnp.float32)
    keep_mask = order_mask[None] * (degree_index[None, :, None] <= degree[:, None, None]).astype(
        jnp.float32
    )
    prepared = prepare(coeffs, keep_mask)
    partial_legendre = legendre_synth(
        prepared.reshape(drop_count * 4, degrees, coef_width), legendre
    )
    surface = fourier_synth(partial_legendre, fourier).reshape(drop_count, 4, nlat, nlon)
    radius, traction_grid = traction(surface, material)
    traction_coeffs = (
        analysis_legendre(analysis_fourier(traction_grid, fourier, quad_weight), legendre)
        * keep_mask
    )
    split_count = split_coeffs.shape[0]
    half_width = split_coeffs.shape[3]
    half_orders = half_width // 2
    half_index = lax.axis_index("row") % 2
    pair_start = (
        lax.axis_index("row") // 2 * lax.axis_size("col") + lax.axis_index("col")
    ) * split_count
    own_material = lax.dynamic_slice_in_dim(split_material, pair_start, split_count, 0)
    own_order = half_index * half_orders + jnp.arange(half_width, dtype=jnp.int32) % half_orders
    keep_half = (degree_index[:, None] >= own_order[None, :]).astype(jnp.float32)
    own_legendre = lax.dynamic_slice_in_dim(legendre, half_index * half_orders, half_orders, 0)
    own_fourier = lax.dynamic_slice_in_dim(
        fourier.reshape(2, degrees, nlon), half_index * half_orders, half_orders, 1
    ).reshape(half_width, nlon)
    split_prepared = prepare(split_coeffs, keep_half[None])
    split_legendre = legendre_synth(
        split_prepared.reshape(split_count * 4, degrees, half_width), own_legendre
    )
    partial_surface = fourier_synth(split_legendre, own_fourier)
    split_surface = partial_surface + from_partner(
        partial_surface.astype(jnp.bfloat16), "row", 0
    ).astype(partial_surface.dtype)
    split_radius, split_grid = traction(
        split_surface.reshape(split_count, 4, nlat, nlon), own_material
    )
    coef_grid = analysis_fourier(split_grid, fourier, quad_weight)
    own_grid = lax.dynamic_slice_in_dim(coef_grid, half_index * half_orders, half_orders, 3)
    split_traction = analysis_legendre(own_grid, own_legendre) * keep_half[None]
    readers = reader_dev.shape[1]
    row_count = lax.axis_size("row")
    col_count = lax.axis_size("col")
    devices = row_count * col_count
    capacity = max(2, 3 * readers * drop_count // (2 * devices))
    cell_count = nlat * nlon
    cell_weight = jnp.broadcast_to(quad_weight[:, None], (nlat, nlon)).reshape(cell_count)
    cell_normal = normals.reshape(3, cell_count)
    near_grid = jnp.stack([radius, traction_grid], axis=1).astype(jnp.bfloat16)
    point_grid = near_grid[:, 0, nlat // 4 :: nlat // 2, :: nlon // 2]
    point_count = point_grid.shape[1] * point_grid.shape[2]
    own_points = point_grid.reshape(drop_count, point_count)
    target_normal = normals[:, nlat // 4 :: nlat // 2, :: nlon // 2].reshape(3, point_count)
    payload = near_grid.reshape(drop_count, 2 * cell_count)
    entry_count = drop_count * readers
    destination = reader_dev.reshape(-1)
    target_slot = reader_slot.reshape(-1)
    onehot = (destination[:, None] == jnp.arange(devices, dtype=jnp.int32)[None, :]).astype(
        jnp.int32
    )
    before = jnp.cumsum(onehot, axis=0) - onehot
    slot_rank = jnp.sum(before * onehot, axis=1)
    position = destination * capacity + slot_rank
    source = jnp.arange(entry_count, dtype=jnp.int32) // readers
    entry_spacing = separation.reshape(3, entry_count)
    slot_count = devices * capacity
    slot_ids = jnp.arange(drop_count, dtype=jnp.int32)
    send_target = jnp.full((slot_count,), -1, jnp.int32).at[position].set(target_slot)

    def near_terms(block_args):
        block_grids, block_spacing, block_points = block_args
        block_rows = block_grids.shape[0]
        source_grid = block_grids.astype(jnp.float32).reshape(block_rows, 2, cell_count)
        return velocity_terms(
            source_grid[:, 0],
            source_grid[:, 1],
            block_spacing,
            block_points.astype(jnp.float32),
            cell_weight,
            cell_normal,
            target_normal,
        )

    got_request = lax.all_to_all(
        send_target.reshape(devices, capacity),
        ("row", "col"),
        split_axis=0,
        concat_axis=0,
        tiled=True,
    ).reshape(slot_count)
    request_pick = (got_request[:, None] == slot_ids[None, :]).astype(jnp.float32)
    answer = jnp.dot(request_pick, own_points.astype(jnp.float32), precision=HIGH).astype(
        jnp.bfloat16
    )
    got_points = lax.all_to_all(
        answer.reshape(devices, capacity, point_count),
        ("row", "col"),
        split_axis=0,
        concat_axis=0,
        tiled=True,
    ).reshape(slot_count, point_count)
    entry_points = got_points[position]
    entry_grids = payload[source]
    block_size = math.gcd(entry_count, 16)
    block_total = entry_count // block_size
    velocity = lax.map(
        near_terms,
        (
            entry_grids.reshape(block_total, block_size, 2 * cell_count),
            jnp.transpose(entry_spacing.reshape(3, block_total, block_size), (1, 0, 2)),
            entry_points.reshape(block_total, block_size, point_count),
        ),
    )
    velocity = jnp.transpose(velocity, (1, 0, 2, 3)).reshape(3, entry_count, point_count)
    send_velocity = (
        jnp.zeros((slot_count, 3, point_count), jnp.float32)
        .at[position]
        .set(jnp.transpose(velocity, (1, 0, 2)))
    )
    got_velocity = lax.all_to_all(
        send_velocity.reshape(devices, capacity, 3 * point_count),
        ("row", "col"),
        split_axis=0,
        concat_axis=0,
        tiled=True,
    )
    near_velocity = jnp.einsum(
        "sd,skp->kdp",
        request_pick,
        got_velocity.reshape(slot_count, 3, point_count),
        precision=HIGH,
    )
    return (traction_coeffs, split_traction, near_velocity.reshape(3, drop_count * point_count))


def solution(mesh):
    in_specs = (
        P(("row", "col"), None, None, None),
        P(("row", "col")),
        P(("row", "col"), None),
        P(("row", "col"), None, None, None),
        P(),
        P(None, ("row", "col"), None),
        P(("row", "col"), None),
        P(("row", "col"), None),
    )
    out_specs = (
        P(("row", "col"), None, None),
        P(("row", "col"), None, None),
        P(None, ("row", "col")),
    )
    return jax.shard_map(
        per_device, mesh=mesh, in_specs=in_specs, out_specs=out_specs, check_vma=False
    )
```

profile of v0, /device:TPU:0, one launch (start us, length us, event | category | flops | bytes accessed | tf_op | source)
XLA Modules:
  0.0 178.0 jit_solution(1115712941768419083)
XLA Ops:
  6.0 7.4 %all-to-all-start = ((s32[32,1,6]{2,1,0:T(1,128)}), s32[32,1,6]{2,1,0:T(1,128)}, u32[]{:S(2)}, u32[]{:S(2)}) async-start(s32[32,1,6]{2,1,0:T(1,128)} %bitcast.33), calls=%async_computation | async-start | bytes 32768 | tf_op jit(solution)/shard_map/all_to_all | solution.py:238
  15.2 1.9 %convolution_bitcast_fusion.3 = f32[16,64,2,32]{1,0,2,3:T(8,128)S(1)} fusion(f32[64,64,64]{2,1,0:T(8,128)S(1)} %copy-done.3, s32[]{:T(128)S(6)} %select_n.80, f32[16,64,2,32]{1,3,2,0:T(8,128)S(1)} %bitcast.174), kind=kOutput, calls=%fused_computation.34 | convolution fusion | flops 50331648 | bytes 1835012 | tf_op jit(solution)/shard_map/mjl,nlcm->njcm/dot_general | solution.py:76
  17.1 2.2 %fusion.66 = (bf16[16,64,128]{2,1,0:T(8,128)(2,1)}, f32[16,64,128]{2,1,0:T(8,128)}) fusion(f32[2,64,128]{2,1,0:T(8,128)S(1)} %copy-done.12, s32[]{:T(128)S(6)} %select_n.80, f32[16,64,2,32]{1,0,2,3:T(8,128)S(1)} %convolution_bitcast_fusion.3), kind=kOutput, calls=%fused_computation.139 | convolution fusion | flops 100794368 | bytes 1343492 | tf_op jit(solution)/shard_map/njw,wk->njk/dot_general | solution.py:81
  19.3 1.7 collective-permute-start
  22.4 3.8 %reshape_reshape.9 = f32[64,64,2,64]{3,2,1,0:T(2,128)} reshape(f32[16,4,64,128]{3,2,1,0:T(8,128)S(1)} %pad_maximum_fusion) | data formatting | bytes 4194304 | tf_op jit(solution)/shard_map/reshape;reshape | solution.py:75
  26.2 7.6 %copy.102 = f32[64,64,2,64]{1,0,2,3:T(8,128)} copy(f32[64,64,2,64]{3,2,1,0:T(2,128)} %reshape_reshape.9) | data formatting | bytes 4194304 | tf_op jit(solution)/shard_map/reshape;reshape | solution.py:75
  33.8 7.0 %convolution_bitcast_fusion = f32[64,64,2,64]{1,0,2,3:T(8,128)} fusion(f32[64,64,2,64]{1,0,2,3:T(8,128)} %copy.102, f32[64,64,64,1]{2,1,3,0:T(8,128)S(1)} %copy-done.2), kind=kOutput, calls=%fused_computation.30 | convolution fusion | flops 402653184 | bytes 5242880 | tf_op jit(solution)/shard_map/mjl,nlcm->njcm/dot_general | solution.py:76
  40.8 7.4 %copy.103 = f32[64,64,2,64]{3,2,1,0:T(2,128)} copy(f32[64,64,2,64]{1,0,2,3:T(8,128)} %convolution_bitcast_fusion) | data formatting | bytes 4194304 | tf_op jit(solution)/shard_map/mjl,nlcm->njcm/transpose | solution.py:76
  48.2 5.4 %dot_general.33 = f32[16,4,64,128]{3,2,1,0:T(8,128)} reshape(f32[64,64,2,64]{3,2,1,0:T(2,128)} %copy.103) | data formatting | bytes 4194304 | tf_op jit(solution)/shard_map/njw,wk->njk/dot_general | solution.py:81
  53.6 3.4 %fusion.67 = f32[16,4,64,128]{3,2,1,0:T(8,128)S(1)} fusion(f32[16,4,64,128]{3,2,1,0:T(8,128)} %dot_general.33, f32[128,128,1,1]{1,0,3,2:T(8,128)S(1)} %copy-done.8), kind=kOutput, calls=%fused_computation.140 | convolution fusion | flops 805306368 | bytes 4259840 | tf_op jit(solution)/shard_map/njw,wk->njk/dot_general | solution.py:81
  57.9 1.4 convolution_multiply_fusion
  59.4 1.6 reshape.304
  61.0 1.4 copy.106
  62.5 3.3 %convolution_bitcast_fusion.1 = f32[16,64,2,64]{1,0,2,3:T(8,128)S(1)} fusion(f32[16,64,2,64]{1,0,2,3:T(8,128)} %copy.106, f32[64,64,64,1]{2,1,3,0:T(8,128)S(1)} %copy-done.2), kind=kOutput, calls=%fused_computation.32 | convolution fusion | flops 100663296 | bytes 2097152 | tf_op jit(solution)/shard_map/mjl,bjcm->blcm/dot_general | solution.py:100
  68.2 1.6 slice.82
  70.4 1.4 reduce.3
  72.8 4.8 %all-to-all-start.1 = ((bf16[32,6,4]{1,2,0:T(4,128)(2,1)}), bf16[32,6,4]{1,2,0:T(4,128)(2,1)S(1)}, u32[]{:S(2)}, u32[]{:S(2)}) async-start(bf16[32,6,4]{1,2,0:T(4,128)(2,1)} %copy.125), calls=%async_computation.1 | async-start | bytes 65536 | tf_op jit(solution)/shard_map/all_to_all | solution.py:249
  78.3 5.1 %gather_fusion = bf16[128,16384]{1,0:T(8,128)(2,1)} fusion(bf16[16,16384]{1,0:T(8,128)(2,1)S(1)} %bitcast.171, s32[1024]{0:T(1024)S(1)} %pad_clamp_fusion.1), kind=kCustom, calls=%fused_computation | custom fusion | bytes 8389120 | tf_op jit(solution)/shard_map/gather | solution.py:257
  83.4 1.3 all-to-all-done.1
  85.9 68.7 %while.12 = (s32[]{:T(128)}, f32[8,3,16,4]{2,3,1,0:T(4,128)S(1)}, bf16[8,16,16384]{2,1,0:T(8,128)(2,1)}, f32[8,3,16]{2,0,1:T(8,128)S(1)}, bf16[8,16,4]{1,2,0:T(4...) while((s32[]{:T(128)}, f32[8,3,16,4]{2,3,1,0:T(4,128)S(1)}, ...), condition=%wide.region_7.8_spmd.clone.clone, body=%wide.region_3.7_spmd.sunk.clone.clone.sunk | while | flops 19399104 | bytes 30786532 | solution.py:260
  86.2 1.1 dynamic-slice_convert_fusion.2
  88.2 1.1 fusion.85
  90.0 1.3 fusion.88
  92.2 2.4 %fusion.90 = f32[3,16,4]{1,2,0:T(4,128)S(1)} fusion(f32[16,4,8192]{2,0,1:T(8,128)S(1)} %get-tuple-element.193, f32[16,4,8192]{2,0,1:T(8,128)S(1)} %get-tuple-element.196, f32[3,8192]{1,0:T(4,128)S(1)} %get-tuple-element.222, f32[16,4,8192]{2,0,1:T(8,128)S(1)} %get-tuple-element.197, f32[3,16,8192]{2,1,0:T(8,128)S(1)} %broadcast_multiply_fusion.8, ...), kind=kLoop, calls=%fused_computation.12.clone.1 | loop fusion | flops 9436992 | bytes 7964160 | tf_op jit(solution)/shard_map/while/body/eval_jaxpr/reduce_sum | solution.py:141
  94.7 1.1 dynamic-slice_convert_fusion.2
  98.6 1.3 fusion.88
  100.7 2.4 %fusion.90 = f32[3,16,4]{1,2,0:T(4,128)S(1)} fusion(f32[16,4,8192]{2,0,1:T(8,128)S(1)} %get-tuple-element.193, f32[16,4,8192]{2,0,1:T(8,128)S(1)} %get-tuple-element.196, f32[3,8192]{1,0:T(4,128)S(1)} %get-tuple-element.222, f32[16,4,8192]{2,0,1:T(8,128)S(1)} %get-tuple-element.197, f32[3,16,8192]{2,1,0:T(8,128)S(1)} %broadcast_multiply_fusion.8, ...), kind=kLoop, calls=%fused_computation.12.clone.1 | loop fusion | flops 9436992 | bytes 7964160 | tf_op jit(solution)/shard_map/while/body/eval_jaxpr/reduce_sum | solution.py:141
  103.3 1.1 dynamic-slice_convert_fusion.2
  107.2 1.3 fusion.88
  109.3 2.4 %fusion.90 = f32[3,16,4]{1,2,0:T(4,128)S(1)} fusion(f32[16,4,8192]{2,0,1:T(8,128)S(1)} %get-tuple-element.193, f32[16,4,8192]{2,0,1:T(8,128)S(1)} %get-tuple-element.196, f32[3,8192]{1,0:T(4,128)S(1)} %get-tuple-element.222, f32[16,4,8192]{2,0,1:T(8,128)S(1)} %get-tuple-element.197, f32[3,16,8192]{2,1,0:T(8,128)S(1)} %broadcast_multiply_fusion.8, ...), kind=kLoop, calls=%fused_computation.12.clone.1 | loop fusion | flops 9436992 | bytes 7964160 | tf_op jit(solution)/shard_map/while/body/eval_jaxpr/reduce_sum | solution.py:141
  111.9 1.1 dynamic-slice_convert_fusion.2
  115.8 1.3 fusion.88
  117.9 2.4 %fusion.90 = f32[3,16,4]{1,2,0:T(4,128)S(1)} fusion(f32[16,4,8192]{2,0,1:T(8,128)S(1)} %get-tuple-element.193, f32[16,4,8192]{2,0,1:T(8,128)S(1)} %get-tuple-element.196, f32[3,8192]{1,0:T(4,128)S(1)} %get-tuple-element.222, f32[16,4,8192]{2,0,1:T(8,128)S(1)} %get-tuple-element.197, f32[3,16,8192]{2,1,0:T(8,128)S(1)} %broadcast_multiply_fusion.8, ...), kind=kLoop, calls=%fused_computation.12.clone.1 | loop fusion | flops 9436992 | bytes 7964160 | tf_op jit(solution)/shard_map/while/body/eval_jaxpr/reduce_sum | solution.py:141
  120.5 1.1 dynamic-slice_convert_fusion.2
  124.3 1.3 fusion.88
  126.5 2.4 %fusion.90 = f32[3,16,4]{1,2,0:T(4,128)S(1)} fusion(f32[16,4,8192]{2,0,1:T(8,128)S(1)} %get-tuple-element.193, f32[16,4,8192]{2,0,1:T(8,128)S(1)} %get-tuple-element.196, f32[3,8192]{1,0:T(4,128)S(1)} %get-tuple-element.222, f32[16,4,8192]{2,0,1:T(8,128)S(1)} %get-tuple-element.197, f32[3,16,8192]{2,1,0:T(8,128)S(1)} %broadcast_multiply_fusion.8, ...), kind=kLoop, calls=%fused_computation.12.clone.1 | loop fusion | flops 9436992 | bytes 7964160 | tf_op jit(solution)/shard_map/while/body/eval_jaxpr/reduce_sum | solution.py:141
  129.0 1.1 dynamic-slice_convert_fusion.2
  132.9 1.3 fusion.88
  135.1 2.4 %fusion.90 = f32[3,16,4]{1,2,0:T(4,128)S(1)} fusion(f32[16,4,8192]{2,0,1:T(8,128)S(1)} %get-tuple-element.193, f32[16,4,8192]{2,0,1:T(8,128)S(1)} %get-tuple-element.196, f32[3,8192]{1,0:T(4,128)S(1)} %get-tuple-element.222, f32[16,4,8192]{2,0,1:T(8,128)S(1)} %get-tuple-element.197, f32[3,16,8192]{2,1,0:T(8,128)S(1)} %broadcast_multiply_fusion.8, ...), kind=kLoop, calls=%fused_computation.12.clone.1 | loop fusion | flops 9436992 | bytes 7964160 | tf_op jit(solution)/shard_map/while/body/eval_jaxpr/reduce_sum | solution.py:141
  137.6 1.1 dynamic-slice_convert_fusion.2
  141.5 1.3 fusion.88
  143.6 2.4 %fusion.90 = f32[3,16,4]{1,2,0:T(4,128)S(1)} fusion(f32[16,4,8192]{2,0,1:T(8,128)S(1)} %get-tuple-element.193, f32[16,4,8192]{2,0,1:T(8,128)S(1)} %get-tuple-element.196, f32[3,8192]{1,0:T(4,128)S(1)} %get-tuple-element.222, f32[16,4,8192]{2,0,1:T(8,128)S(1)} %get-tuple-element.197, f32[3,16,8192]{2,1,0:T(8,128)S(1)} %broadcast_multiply_fusion.8, ...), kind=kLoop, calls=%fused_computation.12.clone.1 | loop fusion | flops 9436992 | bytes 7964160 | tf_op jit(solution)/shard_map/while/body/eval_jaxpr/reduce_sum | solution.py:141
  146.2 1.1 dynamic-slice_convert_fusion.2
  150.1 1.3 fusion.88
  152.2 2.4 %fusion.90 = f32[3,16,4]{1,2,0:T(4,128)S(1)} fusion(f32[16,4,8192]{2,0,1:T(8,128)S(1)} %get-tuple-element.193, f32[16,4,8192]{2,0,1:T(8,128)S(1)} %get-tuple-element.196, f32[3,8192]{1,0:T(4,128)S(1)} %get-tuple-element.222, f32[16,4,8192]{2,0,1:T(8,128)S(1)} %get-tuple-element.197, f32[3,16,8192]{2,1,0:T(8,128)S(1)} %broadcast_multiply_fusion.8, ...), kind=kLoop, calls=%fused_computation.12.clone.1 | loop fusion | flops 9436992 | bytes 7964160 | tf_op jit(solution)/shard_map/while/body/eval_jaxpr/reduce_sum | solution.py:141
  155.0 4.4 %scatter_fusion = f32[192,3,4]{2,1,0:T(4,128)S(1)} fusion(f32[192,3,4]{2,1,0:T(4,128)S(1)} %broadcast_in_dim.9, s32[128]{0:T(128)S(1)} %copy-done.15, f32[128,3,4]{2,1,0:T(4,128)S(1)} %copy.131), kind=kCustom, calls=%fused_computation.3 | custom fusion | bytes 18944 | tf_op jit(solution)/shard_map/scatter | solution.py:272
  160.2 4.3 %all-to-all-start.2 = ((f32[32,6,12]{2,1,0:T(8,128)}), f32[32,6,12]{2,1,0:T(8,128)S(1)}, u32[]{:S(2)}, u32[]{:S(2)}) async-start(f32[32,6,12]{2,1,0:T(8,128)} %reshape.362), calls=%async_computation.2 | async-start | bytes 262144 | tf_op jit(solution)/shard_map/all_to_all | solution.py:274
  164.6 8.2 %all-to-all-done.2 = f32[32,6,12]{2,1,0:T(8,128)S(1)} async-done(((f32[32,6,12]{2,1,0:T(8,128)}), f32[32,6,12]{2,1,0:T(8,128)S(1)}, u32[]{:S(2)}, u32[]{:S(2)}) %all-to-all-start.2) | async-done | bytes 9248 | tf_op jit(solution)/shard_map/all_to_all | solution.py:274
  (200 shorter events, 50.0 us)
Async XLA Ops:
  0.6 77.0 %copy-start = (f32[64,2]{0,1:T(2,128)S(1)}, f32[64,2]{0,1:T(2,128)}, u32[]{:S(2)}) copy-start(f32[64,2]{0,1:T(2,128)} %param.18) | copy-start | bytes 1540
  0.6 14.6 %copy-start.3 = (f32[64,64,64]{2,1,0:T(8,128)S(1)}, f32[64,64,64]{2,1,0:T(8,128)}, u32[]{:S(2)}) copy-start(f32[64,64,64]{2,1,0:T(8,128)} %constant.145.clone) | copy-start | bytes 3145732
  4.3 16.7 %copy-start.14 = (s32[128]{0:T(128)}, s32[128]{0:T(128)S(1)}, u32[]{:S(2)}) copy-start(s32[128]{0:T(128)S(1)} %get-tuple-element.148) | copy-start | bytes 1540
  6.0 63.8 %all-to-all-start = ((s32[32,1,6]{2,1,0:T(1,128)}), s32[32,1,6]{2,1,0:T(1,128)}, u32[]{:S(2)}, u32[]{:S(2)}) async-start(s32[32,1,6]{2,1,0:T(1,128)} %bitcast.33), calls=%async_computation | async-start | bytes 32768 | tf_op jit(solution)/shard_map/all_to_all | solution.py:238
  15.0 2.1 %copy-start.12 = (f32[2,64,128]{2,1,0:T(8,128)S(1)}, f32[2,64,128]{2,1,0:T(8,128)}, u32[]{:S(2)}) copy-start(f32[2,64,128]{2,1,0:T(8,128)} %constant.156) | copy-start | bytes 196612
  15.1 6.5 %copy-start.17 = (f32[16,2]{0,1:T(2,128)S(1)}, f32[16,2]{0,1:T(2,128)}, u32[]{:S(2)}) copy-start(f32[16,2]{0,1:T(2,128)} %param.16) | copy-start | bytes 388
  15.1 6.5 %copy-start.18 = (s32[16]{0:T(128)S(1)}, s32[16]{0:T(128)}, u32[]{:S(2)}) copy-start(s32[16]{0:T(128)} %param.15) | copy-start | bytes 196
  15.1 6.6 %copy-start.6 = (f32[16,3,64,128]{3,2,1,0:T(8,128)S(1)}, f32[16,3,64,128]{3,2,1,0:T(8,128)}, u32[]{:S(2)}) copy-start(f32[16,3,64,128]{3,2,1,0:T(8,128)} %param.14) | copy-start | bytes 4718596
  19.3 154.9 %collective-permute-start = (bf16[16,64,128]{2,1,0:T(8,128)(2,1)}, bf16[16,64,128]{2,1,0:T(8,128)(2,1)}, u32[]{:S(2)}, u32[]{:S(2)}) collective-permute-start(bf16[16,64,128]{2,1,0:T(8,128)(2,1)} %get-tuple-element.145), channel_id=1, source_target_pairs={{0,8},{8,0},{16,24},{24,16},{1,9},{9,1},{17,25},{25,17},{2,10},{10... | collective-permute-start | bytes 786440 | tf_op jit(solution)/shard_map/ppermute | solution.py:20
  26.2 7.6 %copy-start.2 = (f32[64,64,64,1]{2,1,3,0:T(8,128)S(1)}, f32[64,64,64,1]{2,1,3,0:T(8,128)}, u32[]{:S(2)}) copy-start(f32[64,64,64,1]{2,1,3,0:T(8,128)} %constant.164) | copy-start | bytes 3145732
  48.2 5.4 %copy-start.8 = (f32[128,128,1,1]{1,0,3,2:T(8,128)S(1)}, f32[128,128,1,1]{1,0,3,2:T(8,128)}, u32[]{:S(2)}) copy-start(f32[128,128,1,1]{1,0,3,2:T(8,128)} %constant.165) | copy-start | bytes 196612
  57.0 0.9 copy-start.9
  57.0 0.9 copy-start.11
  65.8 2.3 %copy-start.7 = (bf16[16,1,64,128]{3,2,1,0:T(8,128)(2,1)S(1)}, bf16[16,1,64,128]{3,2,1,0:T(8,128)(2,1)}, u32[]{:S(2)}) copy-start(bf16[16,1,64,128]{3,2,1,0:T(8,128)(2,1)} %get-tuple-element.133) | copy-start | bytes 786436
  66.5 1.7 copy-start.16
  66.5 11.3 %copy-start.13 = (f32[3,16,8]{1,2,0:T(8,128)S(1)}, f32[3,16,8]{1,2,0:T(8,128)}, u32[]{:S(2)}) copy-start(f32[3,16,8]{1,2,0:T(8,128)} %param.19) | copy-start | bytes 4612
  72.8 11.9 %all-to-all-start.1 = ((bf16[32,6,4]{1,2,0:T(4,128)(2,1)}), bf16[32,6,4]{1,2,0:T(4,128)(2,1)S(1)}, u32[]{:S(2)}, u32[]{:S(2)}) async-start(bf16[32,6,4]{1,2,0:T(4,128)(2,1)} %copy.125), calls=%async_computation.1 | async-start | bytes 65536 | tf_op jit(solution)/shard_map/all_to_all | solution.py:249
  78.2 7.7 %copy-start.1 = (f32[3,8192]{1,0:T(4,128)S(1)}, f32[3,8192]{1,0:T(4,128)}, u32[]{:S(2)}) copy-start(f32[3,8192]{1,0:T(4,128)} %constant.254) | copy-start | bytes 294916
  78.2 7.7 %copy-start.10 = (f32[3,4]{1,0:T(4,128)S(1)}, f32[3,4]{1,0:T(4,128)}, u32[]{:S(2)}) copy-start(f32[3,4]{1,0:T(4,128)} %constant.255) | copy-start | bytes 148
  85.9 69.0 %copy-start.15 = (s32[128]{0:T(128)S(1)}, s32[128]{0:T(128)}, u32[]{:S(2)}) copy-start(s32[128]{0:T(128)} %copy-done.14) | copy-start | bytes 1540
  154.6 19.6 %copy-start.5 = (f32[16,64,128]{2,1,0:T(8,128)S(1)}, f32[16,64,128]{2,1,0:T(8,128)}, u32[]{:S(2)}) copy-start(f32[16,64,128]{2,1,0:T(8,128)} %get-tuple-element.146) | copy-start | bytes 1572868
  159.3 16.9 %copy-start.4 = (f32[64,64,64]{2,1,0:T(8,128)S(1)}, f32[64,64,64]{2,1,0:T(8,128)}, u32[]{:S(2)}) copy-start(f32[64,64,64]{2,1,0:T(8,128)} %constant.145.clone) | copy-start | bytes 3145732
  160.2 12.6 %all-to-all-start.2 = ((f32[32,6,12]{2,1,0:T(8,128)}), f32[32,6,12]{2,1,0:T(8,128)S(1)}, u32[]{:S(2)}, u32[]{:S(2)}) async-start(f32[32,6,12]{2,1,0:T(8,128)} %reshape.362), calls=%async_computation.2 | async-start | bytes 262144 | tf_op jit(solution)/shard_map/all_to_all | solution.py:274
where the time goes:
time: 179 us; the launch traced here: 178 us
  local copies, waits for them, and re-layouts  68.5 us (38%)
  other arithmetic  59.3 us (33%)
  matrix products  20.7 us (12%)
  starting transfers between devices  18.3 us (10%)
  waiting for transfers between devices  9.5 us (5%)
    reduce_sum x8, other arithmetic, velocity_terms(): return jnp.sum(stokeslet, axis=3) / (8.0 * math.pi)  18.9 us
    div x16, other arithmetic, velocity_terms(): weight = load_grid[:, None, :] / (softened * jnp.sqrt(softened))  11.5 us
    another operation x2, local copies, waits for them, and re-layouts, legendre_synth(): parted = coeff.reshape(batch_size, degrees, 2, orders)  11.4 us
    reduce_sum x8, other arithmetic, velocity_terms(): distance_sq = jnp.sum(offset * offset, axis=0)  10.5 us
    convert_element_type x8, other arithmetic, near_terms(): block_grids.astype(jnp.float32).reshape(block_rows, 2, cell_count)  8.93 us
    dot_general x2, matrix products, legendre_synth(): return jnp.einsum('mjl,nlcm->njcm', legendre, parted, precision=HIGH)  8.9 us
    slice x8, local copies, waits for them, and re-layouts, near_terms(): source_grid[:, 1]  8.86 us
    all_to_all x1, waiting for transfers between devices, per_device(): lax.all_to_all(send_velocity.reshape(devices, capacity, 3 * point_count),...  8.22 us
  transfers between devices with their start and end apart: 4, of which 2 were waited for; matrix products, arithmetic and copies ran while one was open for 78% of the time, Pallas kernels for 0%

commit v1 on v0

v1 whole, which is shorter than its diff:
```python
import functools
import math

import jax
import jax.numpy as jnp
import numpy as np
from jax import lax
from jax.experimental import pallas as pl
from jax.experimental.pallas import tpu as pltpu
from jax.sharding import PartitionSpec as P

SOFTENING = 0.04
LANES = 128
F32 = jnp.float32
BF16 = jnp.bfloat16


def spectral_tables(degrees):
    nlon = 2 * degrees
    theta = (np.arange(degrees) + 0.5) * (math.pi / degrees)
    cosine, sine = np.cos(theta), np.sin(theta)
    legendre = np.zeros((degrees, degrees, degrees))
    for order in range(degrees):
        total = sum(math.log((2.0 * i + 1.0) / (2.0 * i)) for i in range(1, order + 1))
        older = np.exp(0.5 * total + order * np.log(sine)) / math.sqrt(4.0 * math.pi)
        legendre[order, :, order] = older
        if order + 1 < degrees:
            newer = math.sqrt(2.0 * order + 3.0) * cosine * older
            legendre[order, :, order + 1] = newer
            for l in range(order + 2, degrees):
                a = math.sqrt((4.0 * l * l - 1.0) / (l * l - order * order))
                b = math.sqrt(((l - 1.0) ** 2 - order * order) / (4.0 * (l - 1.0) ** 2 - 1.0))
                older, newer = newer, a * (cosine * newer - b * older)
                legendre[order, :, l] = newer
    phase = np.arange(degrees)[:, None] * np.arange(nlon)[None, :] % nlon * (2.0 * math.pi / nlon)
    fourier = np.concatenate([np.cos(phase), np.sin(phase)], axis=0)
    weight = sine * (math.pi / degrees) * (2.0 * math.pi / nlon)
    lon = np.arange(nlon) * (2.0 * math.pi / nlon)
    return legendre, fourier, weight, sine, cosine, lon


def parity_tables(legendre, weight):
    degrees = legendre.shape[0]
    half = degrees // 2
    order = np.arange(2 * degrees) % degrees
    by_lane = legendre[order]
    step = np.arange(half)
    even = np.zeros((half, half, 2 * degrees))
    odd = np.zeros((half, half, 2 * degrees))
    for lane, m in enumerate(order):
        even[:, :, lane] = by_lane[lane][:half, 2 * step + m % 2].T
        odd[:, :, lane] = by_lane[lane][:half, 2 * step + 1 - m % 2].T
    scale = weight[:half, None, None]
    back_even = np.transpose(even, (1, 0, 2)) * scale
    back_odd = np.transpose(odd, (1, 0, 2)) * scale
    return [np.asarray(t, np.float32) for t in (even, odd, back_even, back_odd)]


def spectral_kernel(
    degree_ref, material_ref, coeffs_ref, even_ref, odd_ref, back_even_ref, back_odd_ref,
    fourier_ref, project_ref, weight_ref, out_ref, radius_ref, load_ref,
    field_scr, part_scr, back_scr,
):
    count, fields, degrees, width = coeffs_ref.shape
    half = degrees // 2
    first = pl.program_id(0) * count
    level = lax.broadcasted_iota(jnp.int32, (degrees, width), 0)
    levelf = level.astype(F32)
    curve = levelf * (levelf + 1.0) * (1.0 / (degrees * degrees))
    viscous = (levelf + 2.0) * (6.0 / degrees)
    half_level = lax.broadcasted_iota(jnp.int32, (half, width), 0)
    even_order = lax.broadcasted_iota(jnp.int32, (half, width), 1) % 2 == 0

    def one_drop(d, carry):
        degree = degree_ref[first + d]
        tension = material_ref[2 * (first + d)]
        viscosity = material_ref[2 * (first + d) + 1]
        keep = level <= degree
        shape = jnp.where(keep, coeffs_ref[d, 0], 0.0)
        field_scr[0] = shape
        field_scr[1] = shape * (tension * curve) + jnp.where(
            keep, coeffs_ref[d, 2] * (viscosity * viscous), 0.0
        )
        field_scr[2] = jnp.where(keep, 3.0 * coeffs_ref[d, 1], 0.0)
        for f in range(3):
            low = field_scr[f, pl.ds(0, half, stride=2), :]
            high = field_scr[f, pl.ds(1, half, stride=2), :]
            part_scr[2 * f] = jnp.where(even_order, low, high)
            part_scr[2 * f + 1] = jnp.where(even_order, high, low)
        total = [jnp.zeros((half, width), F32) for _ in range(6)]
        for i in range(half):
            pe, po = even_ref[i], odd_ref[i]
            for f in range(3):
                total[2 * f] = total[2 * f] + pe * part_scr[2 * f, i : i + 1, :]
                total[2 * f + 1] = total[2 * f + 1] + po * part_scr[2 * f + 1, i : i + 1, :]
        rows = []
        for f in range(3):
            rows += [total[2 * f] + total[2 * f + 1], total[2 * f] - total[2 * f + 1]]
        rows = jnp.concatenate(rows, axis=0)
        coarse = rows.astype(BF16)
        fine = (rows - coarse.astype(F32)).astype(BF16)
        f_coarse, f_fine = fourier_ref[0], fourier_ref[1]
        surface = (
            jnp.dot(coarse, f_coarse, preferred_element_type=F32)
            + jnp.dot(fine, f_coarse, preferred_element_type=F32)
            + jnp.dot(coarse, f_fine, preferred_element_type=F32)
        )
        radius = jnp.exp(surface[:degrees])
        potential = surface[2 * degrees :]
        traction = surface[degrees : 2 * degrees] + 0.5 * potential * potential
        radius_ref[d] = radius
        load_ref[d] = traction * radius * radius * weight_ref[...]
        project = jnp.dot(traction.astype(BF16), project_ref[...], preferred_element_type=F32)
        back_scr[0] = project[:half] + project[half:]
        back_scr[1] = project[:half] - project[half:]
        low = jnp.zeros((half, width), F32)
        high = jnp.zeros((half, width), F32)
        for j in range(half):
            low = low + back_even_ref[j] * back_scr[0, j : j + 1, :]
            high = high + back_odd_ref[j] * back_scr[1, j : j + 1, :]
        out_ref[d, pl.ds(0, half, stride=2), :] = jnp.where(
            2 * half_level <= degree, jnp.where(even_order, low, high), 0.0
        )
        out_ref[d, pl.ds(1, half, stride=2), :] = jnp.where(
            2 * half_level + 1 <= degree, jnp.where(even_order, high, low), 0.0
        )
        return carry

    lax.fori_loop(0, count, one_drop, 0)


def spectral(coeffs, degree, material, tables):
    drops, fields, degrees, width = coeffs.shape
    legendre, fourier, weight, sine, cosine, lon = tables
    half = degrees // 2
    block = math.gcd(drops, 4)
    f32 = jnp.asarray(fourier, F32)
    coarse = f32.astype(BF16)
    fourier_parts = jnp.stack([coarse, (f32 - coarse.astype(F32)).astype(BF16)])
    project = jnp.asarray(fourier.T, BF16)
    folded = np.concatenate([weight[:half], weight[:half]]) / (8.0 * math.pi)
    weight_grid = jnp.asarray(np.broadcast_to(folded[:, None], (degrees, width)), F32)
    parity = [jnp.asarray(t) for t in parity_tables(legendre, weight)]
    whole = lambda a: pl.BlockSpec(a.shape, lambda i: (0,) * a.ndim)
    smem = pl.BlockSpec(memory_space=pltpu.SMEM)
    consts = parity + [fourier_parts, project, weight_grid]
    grid_spec = pl.BlockSpec((block, degrees, width), lambda i: (i, 0, 0))
    return pl.pallas_call(
        spectral_kernel,
        grid=(drops // block,),
        in_specs=[smem, smem, pl.BlockSpec((block, fields, degrees, width), lambda i: (i, 0, 0, 0))]
        + [whole(a) for a in consts],
        out_specs=[grid_spec] * 3,
        out_shape=[jax.ShapeDtypeStruct((drops, degrees, width), F32)] * 3,
        scratch_shapes=[
            pltpu.VMEM((3, degrees, width), F32),
            pltpu.VMEM((6, half, width), F32),
            pltpu.VMEM((2, half, width), F32),
        ],
        compiler_params=pltpu.CompilerParams(vmem_limit_bytes=32 << 20),
        cost_estimate=pl.CostEstimate(
            flops=drops * 5_000_000, bytes_accessed=drops * 300_000, transcendentals=drops * 8192
        ),
    )(degree, material.reshape(-1), coeffs, *consts)


def near_kernel(
    normals, index_ref, slot_ref, dest_ref, sep_ref, points_ref, radius_ref, load_ref,
    turn_ref, tilt_ref, out_ref, target_scr, spread_scr,
):
    drops, degrees, width = radius_ref.shape
    entries = index_ref.shape[0]
    readers = entries // drops
    half = degrees // 2
    targets = points_ref.shape[0]
    columns = spread_scr.shape[1]
    point_count = len(normals)
    pick = lax.broadcasted_iota(jnp.int32, (entries, targets), 1) == index_ref[...]
    target_scr[...] = jnp.dot(
        pick.astype(F32).astype(BF16), points_ref[...], preferred_element_type=F32
    )
    lane = lax.broadcasted_iota(jnp.int32, (readers, columns), 1)
    block = drops * point_count
    kind = lane // block * point_count + lane % point_count
    lane_slot = lane % block // point_count

    def one_drop(d, carry):
        rows = pl.ds(pl.multiple_of(d * readers, readers), readers)
        sep = sep_ref[rows, :]
        reach = target_scr[rows, :]
        xs, ring, height, square = [], [], [], []
        for p in range(point_count):
            at = reach[:, p : p + 1]
            x = [
                jnp.broadcast_to(sep[:, c : c + 1] + at * normals[p][c], (readers, width))
                for c in range(3)
            ]
            xs.append(x)
            ring.append(x[0] * turn_ref[0:1, :] + x[1] * turn_ref[1:2, :])
            height.append(x[2])
            square.append(x[0] * x[0] + x[1] * x[1] + x[2] * x[2] + SOFTENING)

        def cell(a, r, rr, h, sq):
            off = a - r
            m = r * off
            t = (sq - rr) - m
            rho = t - m
            inv = lax.rsqrt(rho)
            g = (inv * h) * (inv * inv)
            return g * ((rho - m) + SOFTENING), g * off

        def tile(jt, acc):
            acc = list(acc)
            base = pl.multiple_of(jt * 8, 8)
            for q in range(8):
                j = base + q
                r0 = radius_ref[d, pl.ds(j, 1), :]
                r1 = radius_ref[d, pl.ds(j + half, 1), :]
                h0 = load_ref[d, pl.ds(j, 1), :]
                h1 = load_ref[d, pl.ds(j + half, 1), :]
                s = tilt_ref[0, pl.ds(j, 1), :]
                c = tilt_ref[1, pl.ds(j, 1), :]
                q0, q1 = r0 * r0, r1 * r1
                for p in range(point_count):
                    flat = s * ring[p]
                    up = c * height[p]
                    w0, v0 = cell(flat + up, r0, q0, h0, square[p])
                    w1, v1 = cell(flat - up, r1, q1, h1, square[p])
                    acc[3 * p] = acc[3 * p] + s * (w0 + w1)
                    acc[3 * p + 1] = acc[3 * p + 1] + c * (w0 - w1)
                    acc[3 * p + 2] = acc[3 * p + 2] + (v0 + v1)
            return tuple(acc)

        zero = jnp.zeros((readers, width), F32)
        acc = lax.fori_loop(0, half // 8, tile, (zero,) * (3 * point_count))
        spread = jnp.zeros((readers, columns), F32)
        for p in range(point_count):
            around, up, along = acc[3 * p : 3 * p + 3]
            terms = (around * turn_ref[0:1, :], around * turn_ref[1:2, :], up)
            for c in range(3):
                value = jnp.sum(terms[c] + along * xs[p][c], axis=1, keepdims=True)
                spread = jnp.where(kind == c * point_count + p, value, spread)
        spread_scr[rows, :] = jnp.where(lane_slot == slot_ref[rows, :], spread, 0.0)
        return carry

    lax.fori_loop(0, drops, one_drop, 0)
    devices = out_ref.shape[0]
    to = lax.broadcasted_iota(jnp.int32, (devices, entries), 0) == dest_ref[...]
    to = to.astype(F32).astype(BF16)
    spread = spread_scr[...]
    coarse = spread.astype(BF16)
    fine = (spread - coarse.astype(F32)).astype(BF16)
    out_ref[...] = jnp.dot(to, coarse, preferred_element_type=F32) + jnp.dot(
        to, fine, preferred_element_type=F32
    )


def near(index, slot, dest, sep, points, radius, load, tables, normals, devices, columns):
    legendre, fourier, weight, sine, cosine, lon = tables
    drops, degrees, width = radius.shape
    half = degrees // 2
    turn = jnp.asarray(np.stack([np.cos(lon), np.sin(lon)]), F32)
    tilt = np.stack([sine[:half], cosine[:half]])
    tilt = jnp.asarray(np.broadcast_to(tilt[:, :, None], (2, half, width)), F32)
    entries = index.shape[0]
    return pl.pallas_call(
        functools.partial(near_kernel, normals),
        in_specs=[pl.BlockSpec(memory_space=pltpu.VMEM)] * 9,
        out_specs=pl.BlockSpec(memory_space=pltpu.VMEM),
        out_shape=jax.ShapeDtypeStruct((devices, columns), F32),
        scratch_shapes=[pltpu.VMEM((entries, LANES), F32), pltpu.VMEM((entries, columns), F32)],
        compiler_params=pltpu.CompilerParams(vmem_limit_bytes=32 << 20),
        cost_estimate=pl.CostEstimate(
            flops=entries * 4 * 8192 * 20, bytes_accessed=2_000_000, transcendentals=entries * 32768
        ),
    )(index, slot, dest, sep, points, radius, load, turn, tilt)


def per_device(
    coeffs, degree, material, split_coeffs, split_material, separation, reader_dev, reader_slot
):
    drops, fields, degrees, width = coeffs.shape
    readers = reader_dev.shape[1]
    entries = drops * readers
    row_count, col_count = lax.axis_size("row"), lax.axis_size("col")
    devices = row_count * col_count
    tables = spectral_tables(degrees)
    legendre, fourier, weight, sine, cosine, lon = tables
    nlat, nlon = degrees, 2 * degrees

    lat_points = range(nlat // 4, nlat, nlat // 2)
    lon_points = range(0, nlon, nlon // 2)
    spots = [(j, k) for j in lat_points for k in lon_points]
    normals = [
        (
            float(sine[j] * math.cos(lon[k])),
            float(sine[j] * math.sin(lon[k])),
            float(cosine[j]),
        )
        for j, k in spots
    ]
    order = np.arange(width) % degrees
    basis = jnp.asarray(
        np.stack([legendre[order, j, :].T * fourier[:, k][None, :] for j, k in spots]), F32
    )
    keep = (jnp.arange(degrees, dtype=jnp.int32)[None, :] <= degree[:, None]).astype(F32)
    shape = coeffs[:, 0] * keep[:, :, None]
    points = jnp.exp(jnp.sum(shape[:, None] * basis[None], axis=(2, 3))).astype(BF16)
    all_points = lax.all_gather(points, ("row", "col"), axis=0, tiled=True)

    split_count = split_coeffs.shape[0]
    share = split_count // 2
    half_orders = split_coeffs.shape[3] // 2
    row, col = lax.axis_index("row"), lax.axis_index("col")
    parity = row % 2
    route = [(r, r ^ 1) for r in range(row_count)]
    mine = lax.dynamic_slice_in_dim(split_coeffs, parity * share, share, 0)
    theirs = lax.dynamic_slice_in_dim(split_coeffs, (1 - parity) * share, share, 0)
    came = lax.ppermute(theirs.astype(BF16), "row", route).astype(F32)

    traction_coeffs, radius, load = spectral(coeffs, degree, material, tables)

    wide = (share, fields, degrees, 2, half_orders)
    mine, came = mine.reshape(wide), came.reshape(wide)
    lower = jnp.where(parity == 0, mine, came)
    upper = jnp.where(parity == 0, came, mine)
    full = jnp.stack([lower, upper], axis=4).reshape(share, fields, degrees, width)
    pair_start = (row // 2 * col_count + col) * split_count + parity * share
    own_material = lax.dynamic_slice_in_dim(split_material, pair_start, share, 0)
    top = jnp.full((share,), degrees - 1, jnp.int32)
    split_out, _, _ = spectral(full, top, own_material, tables)
    cut = split_out.reshape(share, degrees, 2, 2, half_orders)
    kept = jnp.where(parity == 0, cut[:, :, :, 0], cut[:, :, :, 1])
    given = jnp.where(parity == 0, cut[:, :, :, 1], cut[:, :, :, 0]).astype(BF16)
    kept = kept.reshape(share, degrees, 2 * half_orders)
    got = lax.ppermute(given.reshape(kept.shape), "row", route).astype(F32)

    point_count = len(spots)
    columns = -(-3 * drops * point_count // LANES) * LANES
    table = jnp.pad(all_points, ((0, 0), (0, LANES - point_count)))
    dest = reader_dev.reshape(1, entries)
    index = (reader_dev * drops + reader_slot).reshape(entries, 1)
    slot = reader_slot.reshape(entries, 1)
    sep = jnp.transpose(separation.reshape(3, entries))
    sent = near(
        index, slot, dest, sep, table, radius, load, tables, normals, devices, columns
    )
    received = lax.all_to_all(sent, ("row", "col"), split_axis=0, concat_axis=0, tiled=True)
    velocity = jnp.sum(received, axis=0)[: 3 * drops * point_count]
    split_traction = jnp.where(
        parity == 0, jnp.concatenate([kept, got]), jnp.concatenate([got, kept])
    )
    return traction_coeffs, split_traction, velocity.reshape(3, drops * point_count)


def solution(mesh):
    both = ("row", "col")
    in_specs = (
        P(both, None, None, None),
        P(both),
        P(both, None),
        P(both, None, None, None),
        P(),
        P(None, both, None),
        P(both, None),
        P(both, None),
    )
    out_specs = (P(both, None, None), P(both, None, None), P(None, both))
    return jax.shard_map(
        per_device, mesh=mesh, in_specs=in_specs, out_specs=out_specs, check_vma=False
    )
```

time: 179 us -> 97 us (0.54)
  local copies, waits for them, and re-layouts: 68.5 us -> 10.4 us
  other arithmetic: 59.3 us -> 4.09 us
  blocking collectives: 0 us -> 40.7 us
  Pallas kernels: 0 us -> 31.5 us
  matrix products: 20.7 us -> 0 us
  starting transfers between devices: 18.3 us -> 7.33 us
  waiting for transfers between devices: 9.5 us -> 1.5 us
    all_gather x0 -> x1, blocking collectives: none -> 40.7 us  [per_device(): all_points = lax.all_gather(points, ('row', 'col'), axis=0, tiled=True)]
    pallas_call x0 -> x3, Pallas kernels: none -> 31.5 us  [the longest x1 16.3 us: near(): pl.pallas_call(functools.partial(near_kernel, normals), in_specs=[pl.Bloc...]
    reduce_sum x17 -> x2, other arithmetic: 29.6 us -> 0.34 us  [the longest x1 0.29 us: per_device(): jnp.sum(shape[:, None] * basis[None], axis=(2, 3))]
    dot_general x10 -> x0, matrix products: 20.7 us -> none  [the longest x2 8.9 us: legendre_synth(): return jnp.einsum('mjl,nlcm->njcm', legendre, parted, precision=HIGH)]
    all_to_all x3 -> x1, starting transfers between devices: 16.6 us -> 2.55 us  [per_device(): lax.all_to_all(sent, ('row', 'col'), split_axis=0, concat_axis=0, tiled=T...]
    slice x11 -> x0, local copies, waits for them, and re-layouts: 11.6 us -> none  [the longest x8 8.86 us: near_terms(): source_grid[:, 1]]
    div x17 -> x0, other arithmetic: 11.5 us -> none  [the longest x16 11.5 us: velocity_terms(): weight = load_grid[:, None, :] / (softened * jnp.sqrt(softened))]
    another operation x3 -> x2, local copies, waits for them, and re-layouts: 11.5 us -> 0.03 us  [the longest x1 0.03 us: per_device(): jnp.stack([lower, upper], axis=4).reshape(share, fields, degrees, width)]
  transfers between devices with their start and end apart: 4 -> 3, of which waited for: 2 -> 2; matrix products, arithmetic and copies ran while one was open for 78% -> 10% of each run, Pallas kernels for 0% -> 33%
where the time goes in v1:
time: 97 us; the launch traced here: 96.5 us
  blocking collectives  40.7 us (42%)
  Pallas kernels  31.5 us (32%)
  local copies, waits for them, and re-layouts  10.4 us (11%)
  starting transfers between devices  7.33 us (8%)
  other arithmetic  4.09 us (4%)
  waiting for transfers between devices  1.5 us (2%)
  between operations  1.01 us (1%)
    all_gather x1, blocking collectives, per_device(): all_points = lax.all_gather(points, ('row', 'col'), axis=0, tiled=True)  40.7 us
    pallas_call x1, Pallas kernels, near(): pl.pallas_call(functools.partial(near_kernel, normals), in_specs=[pl.Bloc...  16.3 us
    pallas_call x2, Pallas kernels, spectral(): pl.pallas_call(spectral_kernel, grid=(drops // block,), in_specs=[smem, s...  15.2 us
    unnamed x40, local copies, waits for them, and re-layouts  7.84 us
    ppermute x1, starting transfers between devices, per_device(): came = lax.ppermute(theirs.astype(BF16), 'row', route).astype(F32)  3.02 us
    all_to_all x1, starting transfers between devices, per_device(): lax.all_to_all(sent, ('row', 'col'), split_axis=0, concat_axis=0, tiled=T...  2.55 us
  transfers between devices with their start and end apart: 3, of which 2 were waited for; matrix products, arithmetic and copies ran while one was open for 10% of the time, Pallas kernels for 33%

profile of v1, /device:TPU:0, one launch (start us, length us, event | category | flops | bytes accessed | tf_op | source)
XLA Modules:
  0.0 96.5 jit_solution(7370200713209881446)
XLA Ops:
  0.6 0.0 copy-start
  0.6 0.0 copy-start.14
  0.7 0.0 copy-start.8
  0.7 0.0 copy-start.2
  0.7 0.0 copy-start.3
  0.7 0.0 copy-start.9
  0.7 0.0 copy-start.10
  0.7 0.0 copy-start.11
  0.8 0.9 copy-done
  1.7 0.8 copy.105
  2.4 3.0 %collective-permute-start = (bf16[2,3,64,64]{2,3,1,0:T(8,128)(2,1)}, bf16[2,3,64,64]{2,3,1,0:T(8,128)(2,1)}, u32[]{:S(2)}, u32[]{:S(2)}) collective-permute-start(bf16[2,3,64,64]{2,3,1,0:T(8,128)(2,1)} %copy.105), channel_id=1, source_target_pairs={{0,8},{8,0},{16,24},{24,16},{1,9},{9,1},{17,25},{25,17},{2,10},{10... | collective-permute-start | bytes 147464 | tf_op jit(solution)/shard_map/ppermute | solution.py:319
  5.4 0.8 copy.96
  6.2 0.7 multiply_add_fusion
  6.9 0.8 copy.95
  7.7 0.1 copy.94
  7.7 0.8 copy.87
  8.5 0.1 reshape.117.material_ref
  8.6 0.7 fusion
  9.3 0.1 reshape.123.dest_ref
  9.4 0.1 reshape.129.slot_ref
  9.5 0.1 reshape.128.index_ref
  9.6 0.8 copy.97
  10.4 1.2 %multiply_bitcast_fusion = f32[16,64,128]{2,1,0:T(8,128)S(1)} fusion(f32[16,3,64,128]{3,2,1,0:T(8,128)} %coeffs_ref.1, f32[16,64]{1,0:T(8,128)S(1)} %fusion), kind=kLoop, calls=%fused_computation.1 | loop fusion | flops 131072 | bytes 1052672 | tf_op jit(solution)/shard_map/mul | solution.py:308
  11.6 0.3 multiply_reduce_fusion
  11.9 0.1 copy.106
  12.0 40.7 %all-gather = bf16[32,16,4]{1,2,0:T(4,128)(2,1)S(1)} all-gather(bf16[1,16,4]{1,2,0:T(4,128)(2,1)S(1)} %bitcast.26), channel_id=1, replica_groups=mesh['row'=4,'col'=8] {'row','col'}, dimensions={0}, use_global_device_ids=true | all-gather | bytes 4224 | tf_op jit(solution)/shard_map/all_gather | solution.py:309
  52.7 0.3 copy.99
  53.1 0.0 copy-start.4
  53.1 1.0 %copy-done.4 = f32[32,32,128]{2,1,0:T(8,128)S(1)} copy-done((f32[32,32,128]{2,1,0:T(8,128)S(1)}, f32[32,32,128]{2,1,0:T(8,128)}, u32[]{:S(2)}) %copy-start.4) | copy-done | bytes 524312
  54.2 1.0 %copy-done.6 = f32[32,32,128]{2,1,0:T(8,128)S(1)} copy-done((f32[32,32,128]{2,1,0:T(8,128)S(1)}, f32[32,32,128]{2,1,0:T(8,128)}, u32[]{:S(2)}) %copy-start.6) | copy-done | bytes 524312
  55.2 12.9 %shard_map.256 = (f32[16,64,128]{2,1,0:T(8,128)}, f32[16,64,128]{2,1,0:T(8,128)S(1)}, f32[16,64,128]{2,1,0:T(8,128)S(1)}) custom-call(s32[16]{0:T(128)S(1)} %copy-done.11, f32[32]{0:T(128)S(1)} %reshape.117.material_ref, f32[16,3,64,128]{3,2,1,0:T(8,128)S(1)} %copy-done.1, f32[32,32,128]{2,1,0:T(8,128)S(1)} %copy-done.6, f32[32,32,128]{2,1,0:T(8,128)S(1)} %copy-done.4, ...), custom_call_target="tpu_custom_call" | custom-call | flops 80000000 | bytes 4800000 | tf_op jit(solution)/shard_map/pallas_call | solution.py:148
  68.1 16.3 %shard_map.258 = f32[32,256]{1,0:T(8,128)S(1)} custom-call(s32[128,1]{1,0:T(8,128)S(1)} %reshape.128.index_ref, s32[128,1]{1,0:T(8,128)S(1)} %reshape.129.slot_ref, s32[1,128]{1,0:T(1,128)S(1)} %reshape.123.dest_ref, f32[128,3]{1,0:T(8,128)S(1)} %bitcast.15, bf16[512,128]{1,0:T(8,128)(2,1)S(1)} %pad.4.points_ref, ...), custom_call_target="tpu_custom_call" | custom-call | flops 83886080 | bytes 2000000 | tf_op jit(solution)/shard_map/pallas_call | solution.py:266
  84.4 0.6 copy.102
  85.1 2.6 %all-to-all-start = ((f32[32,1,256]{2,1,0:T(1,128)}), f32[32,1,256]{2,1,0:T(1,128)S(1)}, u32[]{:S(2)}, u32[]{:S(2)}) async-start(f32[32,1,256]{2,1,0:T(1,128)} %copy.102), calls=%async_computation | async-start | bytes 65536 | tf_op jit(solution)/shard_map/all_to_all | solution.py:348
  87.7 0.1 constant_dynamic-slice_fusion.2
  87.8 0.1 copy.88
  87.9 0.1 reshape.118.material_ref
  88.0 0.1 copy.104
  88.1 1.0 %convert_select_fusion.1 = (f32[2,3,64,64]{2,3,1,0:T(8,128)S(1)}, f32[2,3,64,64]{2,3,1,0:T(8,128)S(1)}) fusion(f32[2,3,64,64]{2,3,1,0:T(8,128)S(1)} %copy.104, bf16[2,3,64,64]{2,3,1,0:T(8,128)(2,1)} %collective-permute-done, pred[]{:T(512)S(6)} %eq.4), kind=kLoop, calls=%fused_computation.4 | loop fusion | flops 73728 | bytes 344065 | tf_op jit(solution)/shard_map/jit(_where)/select_n | solution.py:325
  89.2 0.1 copy.92.coeffs_ref
  89.4 2.3 %shard_map.257 = (f32[2,64,128]{2,1,0:T(8,128)S(1)}, f32[2,64,128]{2,1,0:T(8,128)}, f32[2,64,128]{2,1,0:T(8,128)}) custom-call(s32[2]{0:T(128)S(1)} %broadcast_1_degree_ref.2.degree_ref, f32[4]{0:T(128)S(1)} %reshape.118.material_ref, f32[2,3,64,128]{3,2,1,0:T(8,128)S(1)} %copy.92.coeffs_ref, f32[32,32,128]{2,1,0:T(8,128)S(1)} %copy-done.7, ...), custom_call_target="tpu_custom_call" | custom-call | flops 10000000 | bytes 600000 | tf_op jit(solution)/shard_map/pallas_call | solution.py:148
  91.6 0.1 copy.93
  91.8 1.8 %collective-permute-start.1 = (bf16[2,64,64]{1,2,0:T(8,128)(2,1)S(1)}, bf16[2,64,64]{1,2,0:T(8,128)(2,1)S(1)}, u32[]{:S(2)}, u32[]{:S(2)}) collective-permute-start(bf16[2,64,64]{1,2,0:T(8,128)(2,1)S(1)} %bitcast.24), channel_id=1, source_target_pairs={{0,8},{8,0},{16,24},{24,16},{1,9},{9,1},{17,25},{25,17},{2,10},{10... | collective-permute-start | bytes 49160 | tf_op jit(solution)/shard_map/ppermute | solution.py:336
  93.5 1.4 %all-to-all-done = f32[32,1,256]{2,1,0:T(1,128)S(1)} async-done(((f32[32,1,256]{2,1,0:T(1,128)}), f32[32,1,256]{2,1,0:T(1,128)S(1)}, u32[]{:S(2)}, u32[]{:S(2)}) %all-to-all-start) | async-done | bytes 32800 | tf_op jit(solution)/shard_map/all_to_all | solution.py:348
  94.9 0.1 reduce_sum.19
  94.9 0.7 reshape.125
  95.6 0.1 collective-permute-done.1
  95.8 0.8 copy.103
  (32 shorter events, 0.2 us)
Async XLA Ops:
  0.6 1.0 %copy-start = (f32[4,3,64,64]{3,2,1,0:T(8,128)S(1)}, f32[4,3,64,64]{3,2,1,0:T(8,128)}, u32[]{:S(2)}) copy-start(f32[4,3,64,64]{3,2,1,0:T(8,128)} %param.28) | copy-start | bytes 589828
  0.6 11.0 %copy-start.14 = (f32[4,64,128]{2,1,0:T(8,128)S(1)}, f32[4,64,128]{2,1,0:T(8,128)}, u32[]{:S(2)}) copy-start(f32[4,64,128]{2,1,0:T(8,128)} %constant.68.clone) | copy-start | bytes 393220
  0.7 52.4 %copy-start.8 = (bf16[2,128,128]{2,1,0:T(8,128)(2,1)S(1)}, bf16[2,128,128]{2,1,0:T(8,128)(2,1)}, u32[]{:S(2)}) copy-start(bf16[2,128,128]{2,1,0:T(8,128)(2,1)} %constant.93.fourier_ref) | copy-start | bytes 196612
  0.7 52.4 %copy-start.2 = (f32[32,32,128]{2,1,0:T(8,128)S(1)}, f32[32,32,128]{2,1,0:T(8,128)}, u32[]{:S(2)}) copy-start(f32[32,32,128]{2,1,0:T(8,128)} %constant.75.clone.back_odd_ref) | copy-start | bytes 1572868
  0.7 52.4 %copy-start.3 = (f32[32,32,128]{2,1,0:T(8,128)S(1)}, f32[32,32,128]{2,1,0:T(8,128)}, u32[]{:S(2)}) copy-start(f32[32,32,128]{2,1,0:T(8,128)} %constant.74.clone.back_even_ref) | copy-start | bytes 1572868
  0.7 52.4 %copy-start.9 = (f32[64,128]{1,0:T(8,128)S(1)}, f32[64,128]{1,0:T(8,128)}, u32[]{:S(2)}) copy-start(f32[64,128]{1,0:T(8,128)} %constant.71.clone.weight_ref) | copy-start | bytes 98308
  0.7 52.4 %copy-start.10 = (bf16[128,128]{1,0:T(8,128)(2,1)S(1)}, bf16[128,128]{1,0:T(8,128)(2,1)}, u32[]{:S(2)}) copy-start(bf16[128,128]{1,0:T(8,128)(2,1)} %constant.70.clone.project_ref) | copy-start | bytes 98308
  0.7 52.4 %copy-start.11 = (s32[16]{0:T(128)S(1)}, s32[16]{0:T(128)}, u32[]{:S(2)}) copy-start(s32[16]{0:T(128)} %degree_ref.1) | copy-start | bytes 196
  0.7 52.4 %copy-start.1 = (f32[16,3,64,128]{3,2,1,0:T(8,128)S(1)}, f32[16,3,64,128]{3,2,1,0:T(8,128)}, u32[]{:S(2)}) copy-start(f32[16,3,64,128]{3,2,1,0:T(8,128)} %coeffs_ref.1) | copy-start | bytes 4718596
  2.4 85.7 %collective-permute-start = (bf16[2,3,64,64]{2,3,1,0:T(8,128)(2,1)}, bf16[2,3,64,64]{2,3,1,0:T(8,128)(2,1)}, u32[]{:S(2)}, u32[]{:S(2)}) collective-permute-start(bf16[2,3,64,64]{2,3,1,0:T(8,128)(2,1)} %copy.105), channel_id=1, source_target_pairs={{0,8},{8,0},{16,24},{24,16},{1,9},{9,1},{17,25},{25,17},{2,10},{10... | collective-permute-start | bytes 147464 | tf_op jit(solution)/shard_map/ppermute | solution.py:319
  53.1 1.0 %copy-start.4 = (f32[32,32,128]{2,1,0:T(8,128)S(1)}, f32[32,32,128]{2,1,0:T(8,128)}, u32[]{:S(2)}) copy-start(f32[32,32,128]{2,1,0:T(8,128)} %constant.73.clone.odd_ref) | copy-start | bytes 1572868
  54.2 1.0 %copy-start.6 = (f32[32,32,128]{2,1,0:T(8,128)S(1)}, f32[32,32,128]{2,1,0:T(8,128)}, u32[]{:S(2)}) copy-start(f32[32,32,128]{2,1,0:T(8,128)} %constant.72.clone.even_ref) | copy-start | bytes 1572868
  55.2 12.9 %copy-start.12 = (f32[2,32,128]{2,1,0:T(8,128)S(1)}, f32[2,32,128]{2,1,0:T(8,128)}, u32[]{:S(2)}) copy-start(f32[2,32,128]{2,1,0:T(8,128)} %constant.77.clone.tilt_ref) | copy-start | bytes 98308
  55.2 12.9 %copy-start.13 = (f32[2,128]{1,0:T(2,128)S(1)}, f32[2,128]{1,0:T(2,128)}, u32[]{:S(2)}) copy-start(f32[2,128]{1,0:T(2,128)} %constant.76.clone.turn_ref) | copy-start | bytes 3076
  68.1 19.6 %copy-start.15 = (f32[64,2]{0,1:T(2,128)S(1)}, f32[64,2]{0,1:T(2,128)}, u32[]{:S(2)}) copy-start(f32[64,2]{0,1:T(2,128)} %param.29) | copy-start | bytes 1540
  85.1 9.8 %all-to-all-start = ((f32[32,1,256]{2,1,0:T(1,128)}), f32[32,1,256]{2,1,0:T(1,128)S(1)}, u32[]{:S(2)}, u32[]{:S(2)}) async-start(f32[32,1,256]{2,1,0:T(1,128)} %copy.102), calls=%async_computation | async-start | bytes 65536 | tf_op jit(solution)/shard_map/all_to_all | solution.py:348
  88.0 1.4 %copy-start.5 = (f32[32,32,128]{2,1,0:T(8,128)S(1)}, f32[32,32,128]{2,1,0:T(8,128)}, u32[]{:S(2)}) copy-start(f32[32,32,128]{2,1,0:T(8,128)} %constant.73.clone.odd_ref) | copy-start | bytes 1572868
  88.0 1.4 %copy-start.7 = (f32[32,32,128]{2,1,0:T(8,128)S(1)}, f32[32,32,128]{2,1,0:T(8,128)}, u32[]{:S(2)}) copy-start(f32[32,32,128]{2,1,0:T(8,128)} %constant.72.clone.even_ref) | copy-start | bytes 1572868
  91.8 4.0 %collective-permute-start.1 = (bf16[2,64,64]{1,2,0:T(8,128)(2,1)S(1)}, bf16[2,64,64]{1,2,0:T(8,128)(2,1)S(1)}, u32[]{:S(2)}, u32[]{:S(2)}) collective-permute-start(bf16[2,64,64]{1,2,0:T(8,128)(2,1)S(1)} %bitcast.24), channel_id=1, source_target_pairs={{0,8},{8,0},{16,24},{24,16},{1,9},{9,1},{17,25},{25,17},{2,10},{10... | collective-permute-start | bytes 49160 | tf_op jit(solution)/shard_map/ppermute | solution.py:336

commit v2 on v1

--- a/solution.py
+++ b/solution.py
@@ -13,6 +13,7 @@
 LANES = 128
 F32 = jnp.float32
 BF16 = jnp.bfloat16
+MESH = pl.DeviceIdType.MESH
 
 
 def spectral_tables(degrees):
@@ -59,7 +60,7 @@
 def spectral_kernel(
     degree_ref, material_ref, coeffs_ref, even_ref, odd_ref, back_even_ref, back_odd_ref,
     fourier_ref, project_ref, weight_ref, out_ref, radius_ref, load_ref,
-    field_scr, part_scr, back_scr,
+    field_scr, part_scr, line_scr, back_scr,
 ):
     count, fields, degrees, width = coeffs_ref.shape
     half = degrees // 2
@@ -71,62 +72,75 @@
     half_level = lax.broadcasted_iota(jnp.int32, (half, width), 0)
     even_order = lax.broadcasted_iota(jnp.int32, (half, width), 1) % 2 == 0
 
-    def one_drop(d, carry):
+    for d in range(count):
         degree = degree_ref[first + d]
         tension = material_ref[2 * (first + d)]
         viscosity = material_ref[2 * (first + d) + 1]
         keep = level <= degree
         shape = jnp.where(keep, coeffs_ref[d, 0], 0.0)
-        field_scr[0] = shape
-        field_scr[1] = shape * (tension * curve) + jnp.where(
+        field_scr[d, 0] = shape
+        field_scr[d, 1] = shape * (tension * curve) + jnp.where(
             keep, coeffs_ref[d, 2] * (viscosity * viscous), 0.0
         )
-        field_scr[2] = jnp.where(keep, 3.0 * coeffs_ref[d, 1], 0.0)
+        field_scr[d, 2] = jnp.where(keep, 3.0 * coeffs_ref[d, 1], 0.0)
         for f in range(3):
-            low = field_scr[f, pl.ds(0, half, stride=2), :]
-            high = field_scr[f, pl.ds(1, half, stride=2), :]
-            part_scr[2 * f] = jnp.where(even_order, low, high)
-            part_scr[2 * f + 1] = jnp.where(even_order, high, low)
+            low = field_scr[d, f, pl.ds(0, half, stride=2), :]
+            high = field_scr[d, f, pl.ds(1, half, stride=2), :]
+            part_scr[d, 2 * f] = jnp.where(even_order, low, high)
+            part_scr[d, 2 * f + 1] = jnp.where(even_order, high, low)
+
+    def synth(d, carry):
         total = [jnp.zeros((half, width), F32) for _ in range(6)]
         for i in range(half):
             pe, po = even_ref[i], odd_ref[i]
             for f in range(3):
-                total[2 * f] = total[2 * f] + pe * part_scr[2 * f, i : i + 1, :]
-                total[2 * f + 1] = total[2 * f + 1] + po * part_scr[2 * f + 1, i : i + 1, :]
-        rows = []
+                total[2 * f] = total[2 * f] + pe * part_scr[d, 2 * f, i : i + 1, :]
+                total[2 * f + 1] = total[2 * f + 1] + po * part_scr[d, 2 * f + 1, i : i + 1, :]
         for f in range(3):
-            rows += [total[2 * f] + total[2 * f + 1], total[2 * f] - total[2 * f + 1]]
-        rows = jnp.concatenate(rows, axis=0)
-        coarse = rows.astype(BF16)
-        fine = (rows - coarse.astype(F32)).astype(BF16)
-        f_coarse, f_fine = fourier_ref[0], fourier_ref[1]
-        surface = (
-            jnp.dot(coarse, f_coarse, preferred_element_type=F32)
-            + jnp.dot(fine, f_coarse, preferred_element_type=F32)
-            + jnp.dot(coarse, f_fine, preferred_element_type=F32)
-        )
+            for side in range(2):
+                rows = total[2 * f] - total[2 * f + 1] if side else total[2 * f] + total[2 * f + 1]
+                coarse = rows.astype(BF16)
+                base = pl.multiple_of(((d * 3 + f) * 2 + side) * half, half)
+                line_scr[pl.ds(base, half), :width] = coarse
+                line_scr[pl.ds(base, half), width:] = (rows - coarse.astype(F32)).astype(BF16)
+        return carry
+
+    lax.fori_loop(0, count, synth, 0)
+    for d in range(count):
+        lines = line_scr[d * 3 * degrees : (d + 1) * 3 * degrees, :]
+        surface = jnp.dot(lines, fourier_ref[...], preferred_element_type=F32)
+        surface = surface[:, :width] + surface[:, width:]
         radius = jnp.exp(surface[:degrees])
         potential = surface[2 * degrees :]
         traction = surface[degrees : 2 * degrees] + 0.5 * potential * potential
         radius_ref[d] = radius
         load_ref[d] = traction * radius * radius * weight_ref[...]
         project = jnp.dot(traction.astype(BF16), project_ref[...], preferred_element_type=F32)
-        back_scr[0] = project[:half] + project[half:]
-        back_scr[1] = project[:half] - project[half:]
-        low = jnp.zeros((half, width), F32)
-        high = jnp.zeros((half, width), F32)
+        back_scr[d, 0] = project[:half] + project[half:]
+        back_scr[d, 1] = project[:half] - project[half:]
+    pair = math.gcd(count, 2)
+
+    def analyse(block, carry):
+        total = [jnp.zeros((half, width), F32) for _ in range(2 * pair)]
         for j in range(half):
-            low = low + back_even_ref[j] * back_scr[0, j : j + 1, :]
-            high = high + back_odd_ref[j] * back_scr[1, j : j + 1, :]
-        out_ref[d, pl.ds(0, half, stride=2), :] = jnp.where(
-            2 * half_level <= degree, jnp.where(even_order, low, high), 0.0
-        )
-        out_ref[d, pl.ds(1, half, stride=2), :] = jnp.where(
-            2 * half_level + 1 <= degree, jnp.where(even_order, high, low), 0.0
-        )
-        return carry
-
-    lax.fori_loop(0, count, one_drop, 0)
+            pe, po = back_even_ref[j], back_odd_ref[j]
+            for n in range(pair):
+                d = block * pair + n
+                total[2 * n] = total[2 * n] + pe * back_scr[d, 0, j : j + 1, :]
+                total[2 * n + 1] = total[2 * n + 1] + po * back_scr[d, 1, j : j + 1, :]
+        for n in range(pair):
+            d = block * pair + n
+            degree = degree_ref[first + d]
+            low, high = total[2 * n], total[2 * n + 1]
+            out_ref[d, pl.ds(0, half, stride=2), :] = jnp.where(
+                2 * half_level <= degree, jnp.where(even_order, low, high), 0.0
+            )
+            out_ref[d, pl.ds(1, half, stride=2), :] = jnp.where(
+                2 * half_level + 1 <= degree, jnp.where(even_order, high, low), 0.0
+            )
+        return carry
+
+    lax.fori_loop(0, count // pair, analyse, 0)
 
 
 def spectral(coeffs, degree, material, tables):
@@ -136,7 +150,13 @@
     block = math.gcd(drops, 4)
     f32 = jnp.asarray(fourier, F32)
     coarse = f32.astype(BF16)
-    fourier_parts = jnp.stack([coarse, (f32 - coarse.astype(F32)).astype(BF16)])
+    fine = (f32 - coarse.astype(F32)).astype(BF16)
+    fourier_parts = jnp.concatenate(
+        [
+            jnp.concatenate([coarse, fine], axis=1),
+            jnp.concatenate([coarse, jnp.zeros_like(fine)], axis=1),
+        ]
+    )
     project = jnp.asarray(fourier.T, BF16)
     folded = np.concatenate([weight[:half], weight[:half]]) / (8.0 * math.pi)
     weight_grid = jnp.asarray(np.broadcast_to(folded[:, None], (degrees, width)), F32)
@@ -153,9 +173,10 @@
         out_specs=[grid_spec] * 3,
         out_shape=[jax.ShapeDtypeStruct((drops, degrees, width), F32)] * 3,
         scratch_shapes=[
-            pltpu.VMEM((3, degrees, width), F32),
-            pltpu.VMEM((6, half, width), F32),
-            pltpu.VMEM((2, half, width), F32),
+            pltpu.VMEM((block, 3, degrees, width), F32),
+            pltpu.VMEM((block, 6, half, width), F32),
+            pltpu.VMEM((block * 3 * degrees, 2 * width), BF16),
+            pltpu.VMEM((block, 2, half, width), F32),
         ],
         compiler_params=pltpu.CompilerParams(vmem_limit_bytes=32 << 20),
         cost_estimate=pl.CostEstimate(
@@ -164,18 +185,119 @@
     )(degree, material.reshape(-1), coeffs, *consts)
 
 
+def place(index):
+    col_count = lax.axis_size("col")
+    return (index // col_count, index % col_count)
+
+
+def own_index():
+    return lax.axis_index("row") * lax.axis_size("col") + lax.axis_index("col")
+
+
+def greet(devices, me):
+    barrier = pltpu.get_barrier_semaphore()
+
+    def one(step, carry):
+        pl.semaphore_signal(
+            barrier, inc=1, device_id=place((me + step) % devices), device_id_type=MESH
+        )
+        return carry
+
+    lax.fori_loop(1, devices, one, 0)
+    return barrier
+
+
+def points_kernel(
+    degree_ref, coeffs_ref, basis_ref, out_ref, shape_scr, part_scr, send_scr, land_scr,
+    local_sem, send_sem, recv_sem,
+):
+    devices = out_ref.shape[0]
+    drops, fields, degrees, width = coeffs_ref.shape
+    point_count = basis_ref.shape[0]
+    me = own_index()
+    load = pltpu.make_async_copy(coeffs_ref.at[:, 0], shape_scr, local_sem)
+    load.start()
+    barrier = greet(devices, me)
+    load.wait()
+    level = lax.broadcasted_iota(jnp.int32, (degrees, width), 0)
+    for d in range(drops):
+        shape = jnp.where(level <= degree_ref[d], shape_scr[d], 0.0)
+        for p in range(point_count):
+            part_scr[p, d : d + 1, :] = jnp.sum(shape * basis_ref[p], axis=0, keepdims=True)
+    lane = lax.broadcasted_iota(jnp.int32, (drops, LANES), 1)
+    surface = jnp.zeros((drops, LANES), F32)
+    for p in range(point_count):
+        surface = jnp.where(lane == p, jnp.sum(part_scr[p], axis=1, keepdims=True), surface)
+    send_scr[...] = jnp.exp(surface).astype(BF16)
+    pl.semaphore_wait(barrier, devices - 1)
+
+    def copy(step):
+        return pltpu.make_async_remote_copy(
+            src_ref=send_scr,
+            dst_ref=land_scr.at[me],
+            send_sem=send_sem.at[step],
+            recv_sem=recv_sem.at[step],
+            device_id=place((me + step) % devices),
+            device_id_type=MESH,
+        )
+
+    def begin(step, carry):
+        copy(step).start()
+        return carry
+
+    def finish(step, carry):
+        copy(step).wait()
+        return carry
+
+    lax.fori_loop(1, devices, begin, 0)
+    land_scr[me] = send_scr[...]
+    lax.fori_loop(1, devices, finish, 0)
+    out_ref[...] = land_scr[...]
+
+
+def gather_points(degree, coeffs, basis, devices):
+    drops, fields, degrees, width = coeffs.shape
+    point_count = basis.shape[0]
+    vmem = pl.BlockSpec(memory_space=pltpu.VMEM)
+    return pl.pallas_call(
+        points_kernel,
+        in_specs=[
+            pl.BlockSpec(memory_space=pltpu.SMEM), pl.BlockSpec(memory_space=pl.ANY), vmem
+        ],
+        out_specs=vmem,
+        out_shape=jax.ShapeDtypeStruct((devices, drops, LANES), BF16),
+        scratch_shapes=[
+            pltpu.VMEM((drops, degrees, width), F32),
+            pltpu.VMEM((point_count, drops, width), F32),
+            pltpu.VMEM((drops, LANES), BF16),
+            pltpu.VMEM((devices, drops, LANES), BF16),
+            pltpu.SemaphoreType.DMA,
+            pltpu.SemaphoreType.DMA((devices,)),
+            pltpu.SemaphoreType.DMA((devices,)),
+        ],
+        compiler_params=pltpu.CompilerParams(
+            collective_id=0, has_side_effects=True, vmem_limit_bytes=32 << 20
+        ),
+    )(degree, coeffs, basis)
+
+
 def near_kernel(
-    normals, index_ref, slot_ref, dest_ref, sep_ref, points_ref, radius_ref, load_ref,
-    turn_ref, tilt_ref, out_ref, target_scr, spread_scr,
+    normals, entry_ref, points_ref, radius_ref, load_ref, turn_ref, tilt_ref, out_ref,
+    target_scr, spread_scr, total_scr, send_scr, land_scr, send_sem, recv_sem,
 ):
     drops, degrees, width = radius_ref.shape
-    entries = index_ref.shape[0]
+    devices = land_scr.shape[0]
+    me = own_index()
+    barrier = greet(devices, me)
+    entries = entry_ref.shape[0]
     readers = entries // drops
     half = degrees // 2
     targets = points_ref.shape[0]
     columns = spread_scr.shape[1]
     point_count = len(normals)
-    pick = lax.broadcasted_iota(jnp.int32, (entries, targets), 1) == index_ref[...]
+    to = entry_ref[:, 3:4].astype(jnp.int32)
+    slot = entry_ref[:, 4:5].astype(jnp.int32)
+    pick = lax.broadcasted_iota(jnp.int32, (entries, targets), 1) == to * drops + slot
     target_scr[...] = jnp.dot(
         pick.astype(F32).astype(BF16), points_ref[...], preferred_element_type=F32
     )
@@ -186,7 +308,7 @@
 
     def one_drop(d, carry):
         rows = pl.ds(pl.multiple_of(d * readers, readers), readers)
-        sep = sep_ref[rows, :]
+        sep = entry_ref[rows, :]
         reach = target_scr[rows, :]
         xs, ring, height, square = [], [], [], []
         for p in range(point_count):
@@ -240,40 +362,85 @@
             for c in range(3):
                 value = jnp.sum(terms[c] + along * xs[p][c], axis=1, keepdims=True)
                 spread = jnp.where(kind == c * point_count + p, value, spread)
-        spread_scr[rows, :] = jnp.where(lane_slot == slot_ref[rows, :], spread, 0.0)
+        spread_scr[rows, :] = jnp.where(
+            lane_slot == sep[:, 4:5].astype(jnp.int32), spread, 0.0
+        )
         return carry
 
     lax.fori_loop(0, drops, one_drop, 0)
-    devices = out_ref.shape[0]
-    to = lax.broadcasted_iota(jnp.int32, (devices, entries), 0) == dest_ref[...]
-    to = to.astype(F32).astype(BF16)
+    goes = lax.broadcasted_iota(jnp.int32, (entries, devices), 1) == to
+    goes = goes.astype(F32).astype(BF16)
     spread = spread_scr[...]
     coarse = spread.astype(BF16)
     fine = (spread - coarse.astype(F32)).astype(BF16)
-    out_ref[...] = jnp.dot(to, coarse, preferred_element_type=F32) + jnp.dot(
-        to, fine, preferred_element_type=F32
-    )
-
-
-def near(index, slot, dest, sep, points, radius, load, tables, normals, devices, columns):
+    first = (((0,), (0,)), ((), ()))
+    total_scr[...] = lax.dot_general(
+        goes, coarse, first, preferred_element_type=F32
+    ) + lax.dot_general(goes, fine, first, preferred_element_type=F32)
+
+    def lay(device, carry):
+        send_scr[device] = total_scr[pl.ds(device, 1), :]
+        return carry
+
+    lax.fori_loop(0, devices, lay, 0)
+    pl.semaphore_wait(barrier, devices - 1)
+
+    def copy(step):
+        other = (me + step) % devices
+        return pltpu.make_async_remote_copy(
+            src_ref=send_scr.at[other],
+            dst_ref=land_scr.at[me],
+            send_sem=send_sem.at[step],
+            recv_sem=recv_sem.at[step],
+            device_id=place(other),
+            device_id_type=MESH,
+        )
+
+    def begin(step, carry):
+        copy(step).start()
+        return carry
+
+    def finish(step, carry):
+        copy(step).wait()
+        return carry
+
+    lax.fori_loop(1, devices, begin, 0)
+    land_scr[me] = send_scr[me]
+    lax.fori_loop(1, devices, finish, 0)
+    velocity = jnp.sum(land_scr[...], axis=0)
+    for c in range(3):
+        out_ref[c : c + 1, :] = velocity[:, c * block : (c + 1) * block]
+
+
+def near(entry, points, radius, load, tables, normals, devices, columns):
     legendre, fourier, weight, sine, cosine, lon = tables
     drops, degrees, width = radius.shape
     half = degrees // 2
     turn = jnp.asarray(np.stack([np.cos(lon), np.sin(lon)]), F32)
     tilt = np.stack([sine[:half], cosine[:half]])
     tilt = jnp.asarray(np.broadcast_to(tilt[:, :, None], (2, half, width)), F32)
-    entries = index.shape[0]
+    entries = entry.shape[0]
     return pl.pallas_call(
         functools.partial(near_kernel, normals),
-        in_specs=[pl.BlockSpec(memory_space=pltpu.VMEM)] * 9,
+        in_specs=[pl.BlockSpec(memory_space=pltpu.VMEM)] * 6,
         out_specs=pl.BlockSpec(memory_space=pltpu.VMEM),
-        out_shape=jax.ShapeDtypeStruct((devices, columns), F32),
-        scratch_shapes=[pltpu.VMEM((entries, LANES), F32), pltpu.VMEM((entries, columns), F32)],
-        compiler_params=pltpu.CompilerParams(vmem_limit_bytes=32 << 20),
+        out_shape=jax.ShapeDtypeStruct((3, drops * len(normals)), F32),
+        scratch_shapes=[
+            pltpu.VMEM((entries, LANES), F32),
+            pltpu.VMEM((entries, columns), F32),
+            pltpu.VMEM((devices, columns), F32),
+            pltpu.VMEM((devices, 1, columns), F32),
+            pltpu.VMEM((devices, 1, columns), F32),
+            pltpu.SemaphoreType.DMA((devices,)),
+            pltpu.SemaphoreType.DMA((devices,)),
+        ],
+        compiler_params=pltpu.CompilerParams(
+            collective_id=1, has_side_effects=True, vmem_limit_bytes=32 << 20
+        ),
         cost_estimate=pl.CostEstimate(
             flops=entries * 4 * 8192 * 20, bytes_accessed=2_000_000, transcendentals=entries * 32768
         ),
-    )(index, slot, dest, sep, points, radius, load, turn, tilt)
+    )(entry, points, radius, load, turn, tilt)
 
 
 def per_device(
@@ -303,10 +470,7 @@
     basis = jnp.asarray(
         np.stack([legendre[order, j, :].T * fourier[:, k][None, :] for j, k in spots]), F32
     )
-    keep = (jnp.arange(degrees, dtype=jnp.int32)[None, :] <= degree[:, None]).astype(F32)
-    shape = coeffs[:, 0] * keep[:, :, None]
-    points = jnp.exp(jnp.sum(shape[:, None] * basis[None], axis=(2, 3))).astype(BF16)
-    all_points = lax.all_gather(points, ("row", "col"), axis=0, tiled=True)
+    all_points = gather_points(degree, coeffs, basis, devices)
 
     split_count = split_coeffs.shape[0]
     share = split_count // 2
@@ -337,20 +501,20 @@
 
     point_count = len(spots)
     columns = -(-3 * drops * point_count // LANES) * LANES
-    table = jnp.pad(all_points, ((0, 0), (0, LANES - point_count)))
-    dest = reader_dev.reshape(1, entries)
-    index = (reader_dev * drops + reader_slot).reshape(entries, 1)
-    slot = reader_slot.reshape(entries, 1)
-    sep = jnp.transpose(separation.reshape(3, entries))
-    sent = near(
-        index, slot, dest, sep, table, radius, load, tables, normals, devices, columns
-    )
-    received = lax.all_to_all(sent, ("row", "col"), split_axis=0, concat_axis=0, tiled=True)
-    velocity = jnp.sum(received, axis=0)[: 3 * drops * point_count]
+    entry = jnp.concatenate(
+        [
+            jnp.transpose(separation, (1, 2, 0)),
+            reader_dev.astype(F32)[:, :, None],
+            reader_slot.astype(F32)[:, :, None],
+        ],
+        axis=2,
+    ).reshape(entries, 5)
+    table = all_points.reshape(devices * drops, LANES)
+    velocity = near(entry, table, radius, load, tables, normals, devices, columns)
     split_traction = jnp.where(
         parity == 0, jnp.concatenate([kept, got]), jnp.concatenate([got, kept])
     )
-    return traction_coeffs, split_traction, velocity.reshape(3, drops * point_count)
+    return traction_coeffs, split_traction, velocity
 
 
 def solution(mesh):

time: 97 us -> 68.2 us (0.70)
  blocking collectives: 40.7 us -> 0 us
  Pallas kernels: 31.5 us -> 47.3 us
  starting transfers between devices: 7.33 us -> 3.81 us
  other arithmetic: 4.09 us -> 1.49 us
  waiting for transfers between devices: 1.5 us -> 3.25 us
    all_gather x1 -> x0, blocking collectives: 40.7 us -> none  [per_device(): all_points = lax.all_gather(points, ('row', 'col'), axis=0, tiled=True)]
    pallas_call x0 -> x1, Pallas kernels: none -> 9.31 us  [gather_points(): pl.pallas_call(points_kernel, in_specs=[pl.BlockSpec(memory_space=pltpu.S...]
    pallas_call x1, Pallas kernels: 16.3 us -> 25 us  [near(): pl.pallas_call(functools.partial(near_kernel, normals), in_specs=[pl.Bloc...]
    ppermute x1, waiting for transfers between devices: 0.13 us -> 3.25 us  [per_device(): got = lax.ppermute(given.reshape(kept.shape), 'row', route).astype(F32)]
    all_to_all x1 -> x0, starting transfers between devices: 2.55 us -> none  [per_device(): lax.all_to_all(sent, ('row', 'col'), split_axis=0, concat_axis=0, tiled=T...]
    pallas_call x2, Pallas kernels: 15.2 us -> 12.9 us  [spectral(): pl.pallas_call(spectral_kernel, grid=(drops // block,), in_specs=[smem, s...]
    all_to_all x1 -> x0, waiting for transfers between devices: 1.37 us -> none  [per_device(): lax.all_to_all(sent, ('row', 'col'), split_axis=0, concat_axis=0, tiled=T...]
    mul x1 -> x0, other arithmetic: 1.24 us -> none  [per_device(): shape[:, None] * basis[None]]
  transfers between devices with their start and end apart: 3 -> 2, of which waited for: 2 -> 1; matrix products, arithmetic and copies ran while one was open for 10% -> 7% of each run, Pallas kernels for 33% -> 67%
where the time goes in v2:
time: 68.2 us; the launch traced here: 67.8 us
  Pallas kernels  47.3 us (69%)
  local copies, waits for them, and re-layouts  11 us (16%)
  starting transfers between devices  3.81 us (6%)
  waiting for transfers between devices  3.25 us (5%)
  other arithmetic  1.49 us (2%)
  between operations  0.94 us (1%)
    pallas_call x1, Pallas kernels, near(): pl.pallas_call(functools.partial(near_kernel, normals), in_specs=[pl.Bloc...  25 us
    pallas_call x2, Pallas kernels, spectral(): pl.pallas_call(spectral_kernel, grid=(drops // block,), in_specs=[smem, s...  12.9 us
    pallas_call x1, Pallas kernels, gather_points(): pl.pallas_call(points_kernel, in_specs=[pl.BlockSpec(memory_space=pltpu.S...  9.31 us
    unnamed x37, local copies, waits for them, and re-layouts  8.38 us
    ppermute x1, waiting for transfers between devices, per_device(): got = lax.ppermute(given.reshape(kept.shape), 'row', route).astype(F32)  3.25 us
    ppermute x1, starting transfers between devices, per_device(): came = lax.ppermute(theirs.astype(BF16), 'row', route).astype(F32)  3.09 us
  transfers between devices with their start and end apart: 2, of which 1 were waited for; matrix products, arithmetic and copies ran while one was open for 7% of the time, Pallas kernels for 67%

profile of v2, /device:TPU:0, one launch (start us, length us, event | category | flops | bytes accessed | tf_op | source)
XLA Modules:
  0.0 67.8 jit_solution(6689972336640519116)
XLA Ops:
  0.6 0.0 copy-start
  0.6 0.0 copy-start.12
  0.7 1.0 %copy-done = f32[4,3,64,64]{3,2,1,0:T(8,128)S(1)} copy-done((f32[4,3,64,64]{3,2,1,0:T(8,128)S(1)}, f32[4,3,64,64]{3,2,1,0:T(8,128)}, u32[]{:S(2)}) %copy-start) | copy-done | bytes 196632
  1.7 0.0 copy-start.3
  1.7 0.0 copy-start.4
  1.7 0.0 copy-start.9
  1.7 0.0 copy-start.10
  1.7 0.0 copy-start.11
  1.7 0.1 copy.75
  1.8 3.1 %collective-permute-start = (bf16[2,3,64,64]{2,3,1,0:T(8,128)(2,1)S(1)}, bf16[2,3,64,64]{2,3,1,0:T(8,128)(2,1)S(1)}, u32[]{:S(2)}, u32[]{:S(2)}) collective-permute-start(bf16[2,3,64,64]{2,3,1,0:T(8,128)(2,1)S(1)} %copy.75), channel_id=1, source_target_pairs={{0,8},{8,0},{16,24},{24,16},{1,9},{9,1},{17,25},{25,17},{2,10},{10... | collective-permute-start | bytes 147464 | tf_op jit(solution)/shard_map/ppermute | solution.py:483
  4.9 0.7 %convert_element_type.51 = f32[16,8]{0,1:T(8,128)S(1)} convert(s32[16,8]{0,1:T(8,128)} %param.31) | non-fusion elementwise | flops 128 | bytes 1024 | tf_op jit(solution)/shard_map/convert_element_type | solution.py:507
  5.6 0.1 copy.70
  5.7 0.1 concatenate.43
  5.8 0.7 %convert_element_type.52 = f32[16,8]{0,1:T(8,128)S(1)} convert(s32[16,8]{0,1:T(8,128)} %param.32) | non-fusion elementwise | flops 128 | bytes 1024 | tf_op jit(solution)/shard_map/convert_element_type | solution.py:508
  6.5 0.1 copy.71
  6.6 0.1 concatenate.44
  6.6 0.8 %copy.69 = f32[16,8,3]{1,0,2:T(8,128)S(1)} copy(f32[16,8,3]{0,1,2:T(8,128)} %bitcast.18) | data formatting | bytes 3072 | tf_op jit(solution)/shard_map/transpose | solution.py:506
  7.4 0.1 concatenate.42
  7.6 0.8 %constant_dynamic-slice_fusion.2 = f32[2,2]{0,1:T(2,128)S(1)} fusion(f32[64,2]{0,1:T(2,128)} %param.29, s32[]{:T(128)S(6)} %select_n.82), kind=kLoop, calls=%fused_computation.9 | loop fusion | bytes 36 | tf_op jit(solution)/shard_map/dynamic_slice | solution.py:493
  8.3 0.1 copy.63
  8.4 0.1 reshape.79.material_ref
  8.5 0.8 %copy.62 = f32[16,2]{1,0:T(8,128)S(1)} copy(f32[16,2]{0,1:T(2,128)} %param.27) | data formatting | bytes 256 | tf_op args[2]
  9.3 0.1 reshape.78.material_ref
  9.4 0.1 copy.72.entry_ref
  9.5 0.1 copy.74
  9.6 0.0 copy-start.1
  9.6 1.4 %copy-done.1 = f32[16,3,64,128]{3,2,1,0:T(8,128)S(1)} copy-done((f32[16,3,64,128]{3,2,1,0:T(8,128)S(1)}, f32[16,3,64,128]{3,2,1,0:T(8,128)}, u32[]{:S(2)}) %copy-start.1) | copy-done | bytes 1572888
  11.0 0.7 copy-done.13
  11.7 9.3 %shard_map.258 = bf16[32,16,128]{2,1,0:T(8,128)(2,1)S(1)} custom-call(s32[16]{0:T(128)S(1)} %copy-done.13, f32[16,3,64,128]{3,2,1,0:T(8,128)S(1)} %copy-done.1, f32[4,64,128]{2,1,0:T(8,128)S(1)} %copy-done.12), custom_call_target="tpu_custom_call" | custom-call | tf_op jit(solution)/shard_map/pallas_call | solution.py:262
  21.0 0.0 copy-done.3
  21.0 0.0 copy-done.4
  21.0 0.0 copy-start.5
  21.1 1.0 %copy-done.5 = f32[32,32,128]{2,1,0:T(8,128)S(1)} copy-done((f32[32,32,128]{2,1,0:T(8,128)S(1)}, f32[32,32,128]{2,1,0:T(8,128)}, u32[]{:S(2)}) %copy-start.5) | copy-done | bytes 524312
  22.1 1.0 %copy-done.7 = f32[32,32,128]{2,1,0:T(8,128)S(1)} copy-done((f32[32,32,128]{2,1,0:T(8,128)S(1)}, f32[32,32,128]{2,1,0:T(8,128)}, u32[]{:S(2)}) %copy-start.7) | copy-done | bytes 524312
  23.1 10.8 %shard_map.256 = (f32[16,64,128]{2,1,0:T(8,128)}, f32[16,64,128]{2,1,0:T(8,128)S(1)}, f32[16,64,128]{2,1,0:T(8,128)S(1)}) custom-call(s32[16]{0:T(128)S(1)} %copy-done.13, f32[32]{0:T(128)S(1)} %reshape.78.material_ref, f32[16,3,64,128]{3,2,1,0:T(8,128)S(1)} %copy-done.2, f32[32,32,128]{2,1,0:T(8,128)S(1)} %copy-done.7, f32[32,32,128]{2,1,0:T(8,128)S(1)} %copy-done.5, ...), custom_call_target="tpu_custom_call" | custom-call | flops 80000000 | bytes 4800000 | tf_op jit(solution)/shard_map/pallas_call | solution.py:168
  34.0 25.0 %shard_map.259 = f32[3,64]{1,0:T(4,128)S(1)} custom-call(f32[128,5]{1,0:T(8,128)S(1)} %copy.72.entry_ref, bf16[512,128]{1,0:T(8,128)(2,1)S(1)} %bitcast.10, f32[16,64,128]{2,1,0:T(8,128)S(1)} %get-tuple-element.9.radius_ref, f32[16,64,128]{2,1,0:T(8,128)S(1)} %get-tuple-element.10.load_ref, f32[2,128]{1,0:T(2,128)S(1)} %copy-done.15, ...), custom_call_target="tpu_custom_call" | custom-call | flops 83886080 | bytes 2000000 | tf_op jit(solution)/shard_map/pallas_call | solution.py:423
  59.0 0.0 copy-start.6
  59.0 0.0 copy-start.8
  59.0 0.0 collective-permute-done
  59.1 0.1 copy.67.coeffs_ref
  59.3 0.7 %copy-done.6 = f32[32,32,128]{2,1,0:T(8,128)S(1)} copy-done((f32[32,32,128]{2,1,0:T(8,128)S(1)}, f32[32,32,128]{2,1,0:T(8,128)}, u32[]{:S(2)}) %copy-start.6) | copy-done | bytes 524312
  60.0 0.2 copy-done.8
  60.2 2.1 %shard_map.257 = (f32[2,64,128]{2,1,0:T(8,128)S(1)}, f32[2,64,128]{2,1,0:T(8,128)}, f32[2,64,128]{2,1,0:T(8,128)}) custom-call(s32[2]{0:T(128)S(1)} %broadcast_2_degree_ref.2.degree_ref, f32[4]{0:T(128)S(1)} %reshape.79.material_ref, f32[2,3,64,128]{3,2,1,0:T(8,128)S(1)} %copy.67.coeffs_ref, f32[32,32,128]{2,1,0:T(8,128)S(1)} %copy-done.8, ...), custom_call_target="tpu_custom_call" | custom-call | flops 10000000 | bytes 600000 | tf_op jit(solution)/shard_map/pallas_call | solution.py:168
  62.3 0.1 copy.68
  62.4 0.7 %collective-permute-start.1 = (bf16[2,64,64]{1,2,0:T(8,128)(2,1)S(1)}, bf16[2,64,64]{1,2,0:T(8,128)(2,1)S(1)}, u32[]{:S(2)}, u32[]{:S(2)}) collective-permute-start(bf16[2,64,64]{1,2,0:T(8,128)(2,1)S(1)} %bitcast.17), channel_id=1, source_target_pairs={{0,8},{8,0},{16,24},{24,16},{1,9},{9,1},{17,25},{25,17},{2,10},{10... | collective-permute-start | bytes 49160 | tf_op jit(solution)/shard_map/ppermute | solution.py:500
  63.2 3.2 %collective-permute-done.1 = bf16[2,64,64]{1,2,0:T(8,128)(2,1)S(1)} collective-permute-done((bf16[2,64,64]{1,2,0:T(8,128)(2,1)S(1)}, bf16[2,64,64]{1,2,0:T(8,128)(2,1)S(1)}, u32[]{:S(2)}, u32[]{:S(2)}) %collective-permute-start.1) | collective-permute-done | bytes 16416 | tf_op jit(solution)/shard_map/ppermute | solution.py:500
  66.4 0.8 %copy.73 = f32[4,64,64]{2,1,0:T(8,128)} copy(f32[4,64,64]{1,2,0:T(8,128)S(1)} %maximum_select_fusion) | data formatting | bytes 131072
  67.2 0.6 copy.77
  (23 shorter events, 0.2 us)
Async XLA Ops:
  0.6 1.0 %copy-start = (f32[4,3,64,64]{3,2,1,0:T(8,128)S(1)}, f32[4,3,64,64]{3,2,1,0:T(8,128)}, u32[]{:S(2)}) copy-start(f32[4,3,64,64]{3,2,1,0:T(8,128)} %param.28) | copy-start | bytes 589828
  0.6 8.9 %copy-start.12 = (f32[4,64,128]{2,1,0:T(8,128)S(1)}, f32[4,64,128]{2,1,0:T(8,128)}, u32[]{:S(2)}) copy-start(f32[4,64,128]{2,1,0:T(8,128)} %constant.64.clone.basis_ref) | copy-start | bytes 393220
  1.7 19.3 %copy-start.3 = (f32[32,32,128]{2,1,0:T(8,128)S(1)}, f32[32,32,128]{2,1,0:T(8,128)}, u32[]{:S(2)}) copy-start(f32[32,32,128]{2,1,0:T(8,128)} %constant.71.clone.back_odd_ref) | copy-start | bytes 1572868
  1.7 19.3 %copy-start.4 = (f32[32,32,128]{2,1,0:T(8,128)S(1)}, f32[32,32,128]{2,1,0:T(8,128)}, u32[]{:S(2)}) copy-start(f32[32,32,128]{2,1,0:T(8,128)} %constant.70.clone.back_even_ref) | copy-start | bytes 1572868
  1.7 19.3 %copy-start.9 = (bf16[256,256]{1,0:T(8,128)(2,1)S(1)}, bf16[256,256]{1,0:T(8,128)(2,1)}, u32[]{:S(2)}) copy-start(bf16[256,256]{1,0:T(8,128)(2,1)} %constant.91.fourier_ref) | copy-start | bytes 393220
  1.7 19.3 %copy-start.10 = (f32[64,128]{1,0:T(8,128)S(1)}, f32[64,128]{1,0:T(8,128)}, u32[]{:S(2)}) copy-start(f32[64,128]{1,0:T(8,128)} %constant.67.clone.weight_ref) | copy-start | bytes 98308
  1.7 19.3 %copy-start.11 = (bf16[128,128]{1,0:T(8,128)(2,1)S(1)}, bf16[128,128]{1,0:T(8,128)(2,1)}, u32[]{:S(2)}) copy-start(bf16[128,128]{1,0:T(8,128)(2,1)} %constant.66.clone.project_ref) | copy-start | bytes 98308
  1.8 57.2 %collective-permute-start = (bf16[2,3,64,64]{2,3,1,0:T(8,128)(2,1)S(1)}, bf16[2,3,64,64]{2,3,1,0:T(8,128)(2,1)S(1)}, u32[]{:S(2)}, u32[]{:S(2)}) collective-permute-start(bf16[2,3,64,64]{2,3,1,0:T(8,128)(2,1)S(1)} %copy.75), channel_id=1, source_target_pairs={{0,8},{8,0},{16,24},{24,16},{1,9},{9,1},{17,25},{25,17},{2,10},{10... | collective-permute-start | bytes 147464 | tf_op jit(solution)/shard_map/ppermute | solution.py:483
  9.6 1.4 %copy-start.1 = (f32[16,3,64,128]{3,2,1,0:T(8,128)S(1)}, f32[16,3,64,128]{3,2,1,0:T(8,128)}, u32[]{:S(2)}) copy-start(f32[16,3,64,128]{3,2,1,0:T(8,128)} %coeffs_ref.3) | copy-start | bytes 4718596
  11.0 0.7 copy-start.13
  11.7 9.4 %copy-start.2 = (f32[16,3,64,128]{3,2,1,0:T(8,128)S(1)}, f32[16,3,64,128]{3,2,1,0:T(8,128)}, u32[]{:S(2)}) copy-start(f32[16,3,64,128]{3,2,1,0:T(8,128)} %coeffs_ref.3) | copy-start | bytes 4718596
  21.0 1.0 %copy-start.5 = (f32[32,32,128]{2,1,0:T(8,128)S(1)}, f32[32,32,128]{2,1,0:T(8,128)}, u32[]{:S(2)}) copy-start(f32[32,32,128]{2,1,0:T(8,128)} %constant.69.clone.odd_ref) | copy-start | bytes 1572868
  22.1 1.0 %copy-start.7 = (f32[32,32,128]{2,1,0:T(8,128)S(1)}, f32[32,32,128]{2,1,0:T(8,128)}, u32[]{:S(2)}) copy-start(f32[32,32,128]{2,1,0:T(8,128)} %constant.68.clone.even_ref) | copy-start | bytes 1572868
  23.1 10.8 %copy-start.14 = (f32[2,32,128]{2,1,0:T(8,128)S(1)}, f32[2,32,128]{2,1,0:T(8,128)}, u32[]{:S(2)}) copy-start(f32[2,32,128]{2,1,0:T(8,128)} %constant.73.clone.tilt_ref) | copy-start | bytes 98308
  23.1 10.8 %copy-start.15 = (f32[2,128]{1,0:T(2,128)S(1)}, f32[2,128]{1,0:T(2,128)}, u32[]{:S(2)}) copy-start(f32[2,128]{1,0:T(2,128)} %constant.72.clone.turn_ref) | copy-start | bytes 3076
  59.0 1.0 %copy-start.6 = (f32[32,32,128]{2,1,0:T(8,128)S(1)}, f32[32,32,128]{2,1,0:T(8,128)}, u32[]{:S(2)}) copy-start(f32[32,32,128]{2,1,0:T(8,128)} %constant.69.clone.odd_ref) | copy-start | bytes 1572868
  59.0 1.2 %copy-start.8 = (f32[32,32,128]{2,1,0:T(8,128)S(1)}, f32[32,32,128]{2,1,0:T(8,128)}, u32[]{:S(2)}) copy-start(f32[32,32,128]{2,1,0:T(8,128)} %constant.68.clone.even_ref) | copy-start | bytes 1572868
  62.4 4.0 %collective-permute-start.1 = (bf16[2,64,64]{1,2,0:T(8,128)(2,1)S(1)}, bf16[2,64,64]{1,2,0:T(8,128)(2,1)S(1)}, u32[]{:S(2)}, u32[]{:S(2)}) collective-permute-start(bf16[2,64,64]{1,2,0:T(8,128)(2,1)S(1)} %bitcast.17), channel_id=1, source_target_pairs={{0,8},{8,0},{16,24},{24,16},{1,9},{9,1},{17,25},{25,17},{2,10},{10... | collective-permute-start | bytes 49160 | tf_op jit(solution)/shard_map/ppermute | solution.py:500

commit v3 on v2

--- a/solution.py
+++ b/solution.py
@@ -57,14 +57,60 @@
     return [np.asarray(t, np.float32) for t in (even, odd, back_even, back_odd)]
 
 
-def spectral_kernel(
-    degree_ref, material_ref, coeffs_ref, even_ref, odd_ref, back_even_ref, back_odd_ref,
-    fourier_ref, project_ref, weight_ref, out_ref, radius_ref, load_ref,
-    field_scr, part_scr, line_scr, back_scr,
-):
+def peers():
+    rows, cols = lax.axis_size("row"), lax.axis_size("col")
+    row, col = lax.axis_index("row"), lax.axis_index("col")
+    result = []
+    for step in range(1, rows * cols):
+        r, c = row + step // cols, col + step % cols
+        result.append((jnp.where(r >= rows, r - rows, r), jnp.where(c >= cols, c - cols, c)))
+    return result
+
+
+def own_index():
+    return lax.axis_index("row") * lax.axis_size("col") + lax.axis_index("col")
+
+
+def greet():
+    barrier = pltpu.get_barrier_semaphore()
+    for peer in peers():
+        pl.semaphore_signal(barrier, inc=1, device_id=peer, device_id_type=MESH)
+    return barrier
+
+
+def to_all(source, land, send_sem, recv_sem):
+    copies = []
+    for n, peer in enumerate(peers()):
+        copies.append(
+            pltpu.make_async_remote_copy(
+                src_ref=source(peer),
+                dst_ref=land.at[own_index()],
+                send_sem=send_sem.at[n],
+                recv_sem=recv_sem.at[n],
+                device_id=peer,
+                device_id_type=MESH,
+            )
+        )
+    return copies
+
+
+def to_partner(source, land, send_sem, recv_sem):
+    row = lax.axis_index("row")
+    return pltpu.make_async_remote_copy(
+        src_ref=source,
+        dst_ref=land,
+        send_sem=send_sem,
+        recv_sem=recv_sem,
+        device_id=(row + 1 - 2 * (row % 2), lax.axis_index("col")),
+        device_id_type=MESH,
+    )
+
+
+def spectral_body(coeffs_ref, scalars, consts, out_ref, radius_ref, load_ref, scratch):
+    even_ref, odd_ref, back_even_ref, back_odd_ref, fourier_ref, project_ref, weight_ref = consts
+    field_scr, part_scr, line_scr, back_scr = scratch
     count, fields, degrees, width = coeffs_ref.shape
     half = degrees // 2
-    first = pl.program_id(0) * count
     level = lax.broadcasted_iota(jnp.int32, (degrees, width), 0)
     levelf = level.astype(F32)
     curve = levelf * (levelf + 1.0) * (1.0 / (degrees * degrees))
@@ -73,9 +119,7 @@
     even_order = lax.broadcasted_iota(jnp.int32, (half, width), 1) % 2 == 0
 
     for d in range(count):
-        degree = degree_ref[first + d]
-        tension = material_ref[2 * (first + d)]
-        viscosity = material_ref[2 * (first + d) + 1]
+        degree, tension, viscosity = scalars(d)
         keep = level <= degree
         shape = jnp.where(keep, coeffs_ref[d, 0], 0.0)
         field_scr[d, 0] = shape
@@ -110,11 +154,12 @@
         lines = line_scr[d * 3 * degrees : (d + 1) * 3 * degrees, :]
         surface = jnp.dot(lines, fourier_ref[...], preferred_element_type=F32)
         surface = surface[:, :width] + surface[:, width:]
-        radius = jnp.exp(surface[:degrees])
         potential = surface[2 * degrees :]
         traction = surface[degrees : 2 * degrees] + 0.5 * potential * potential
-        radius_ref[d] = radius
-        load_ref[d] = traction * radius * radius * weight_ref[...]
+        if radius_ref is not None:
+            radius = jnp.exp(surface[:degrees])
+            radius_ref[d] = radius
+            load_ref[d] = traction * radius * radius * weight_ref[...]
         project = jnp.dot(traction.astype(BF16), project_ref[...], preferred_element_type=F32)
         back_scr[d, 0] = project[:half] + project[half:]
         back_scr[d, 1] = project[:half] - project[half:]
@@ -130,7 +175,7 @@
                 total[2 * n + 1] = total[2 * n + 1] + po * back_scr[d, 1, j : j + 1, :]
         for n in range(pair):
             d = block * pair + n
-            degree = degree_ref[first + d]
+            degree = scalars(d)[0]
             low, high = total[2 * n], total[2 * n + 1]
             out_ref[d, pl.ds(0, half, stride=2), :] = jnp.where(
                 2 * half_level <= degree, jnp.where(even_order, low, high), 0.0
@@ -143,11 +188,96 @@
     lax.fori_loop(0, count // pair, analyse, 0)
 
 
-def spectral(coeffs, degree, material, tables):
+def spectral_kernel(
+    degree_ref, material_ref, split_material_ref, coeffs_ref, all_coeffs_ref, split_ref, basis_ref,
+    *rest,
+):
+    consts, rest = rest[:7], rest[7:]
+    out_ref, radius_ref, load_ref, split_out_ref, points_ref = rest[:5]
+    scratch, rest = rest[5:9], rest[9:]
+    (shape_scr, point_scr, send_scr, land_scr, give_scr, came_scr, full_scr,
+     local_sem, send_sem, recv_sem, give_sem, came_sem) = rest
+    count, fields, degrees, width = coeffs_ref.shape
+    drops = shape_scr.shape[0]
+    split_count, half_width = split_ref.shape[0], split_ref.shape[3]
+    share, orders = split_count // 2, half_width // 2
+    devices = land_scr.shape[0]
+    steps = drops // count
+    step = pl.program_id(0)
+    row, col = lax.axis_index("row"), lax.axis_index("col")
+    parity = row % 2
+    local = pltpu.make_async_copy(all_coeffs_ref.at[:, 0], shape_scr, local_sem)
+    swap = to_partner(give_scr, came_scr, give_sem, came_sem)
+
+    @pl.when(step == 0)
+    def _():
+        local.start()
+        greet()
+        give_scr[...] = split_ref[pl.ds((1 - parity) * share, share)].astype(BF16)
+
+    @pl.when(step < steps)
+    def _():
+        first = step * count
+
+        def scalars(d):
+            at = first + d
+            return degree_ref[at], material_ref[0, at], material_ref[1, at]
+
+        spectral_body(coeffs_ref, scalars, consts, out_ref, radius_ref, load_ref, scratch)
+
+    @pl.when(step == 0)
+    def _():
+        local.wait()
+        level = lax.broadcasted_iota(jnp.int32, (degrees, width), 0)
+        point_count = basis_ref.shape[0]
+        for d in range(drops):
+            shape = jnp.where(level <= degree_ref[d], shape_scr[d], 0.0)
+            for p in range(point_count):
+                point_scr[p, d : d + 1, :] = jnp.sum(shape * basis_ref[p], axis=0, keepdims=True)
+        lane = lax.broadcasted_iota(jnp.int32, (drops, LANES), 1)
+        surface = jnp.zeros((drops, LANES), F32)
+        for p in range(point_count):
+            surface = jnp.where(lane == p, jnp.sum(point_scr[p], axis=1, keepdims=True), surface)
+        send_scr[...] = jnp.exp(surface).astype(BF16)
+        pl.semaphore_wait(pltpu.get_barrier_semaphore(), devices - 1)
+        swap.start()
+        for copy in to_all(lambda peer: send_scr, land_scr, send_sem, recv_sem):
+            copy.start()
+        land_scr[own_index()] = send_scr[...]
+
+    @pl.when(step == steps)
+    def _():
+        swap.wait()
+        mine = split_ref[pl.ds(parity * share, share)]
+        came = came_scr[...].astype(F32)
+        for d in range(share):
+            for f in range(fields):
+                lower = jnp.where(parity == 0, mine[d, f], came[d, f])
+                upper = jnp.where(parity == 0, came[d, f], mine[d, f])
+                full_scr[d, f] = jnp.concatenate(
+                    [lower[:, :orders], upper[:, :orders], lower[:, orders:], upper[:, orders:]],
+                    axis=1,
+                )
+        start = (row // 2 * lax.axis_size("col") + col) * split_count + parity * share
+
+        def scalars(d):
+            at = start + d
+            return degrees - 1, split_material_ref[0, at], split_material_ref[1, at]
+
+        spectral_body(full_scr, scalars, consts, split_out_ref, None, None, scratch)
+        for copy in to_all(lambda peer: send_scr, land_scr, send_sem, recv_sem):
+            copy.wait()
+        points_ref[...] = land_scr[...]
+
+
+def spectral(coeffs, degree, material, split_coeffs, split_material, basis, tables, devices):
     drops, fields, degrees, width = coeffs.shape
+    split_count, half_width = split_coeffs.shape[0], split_coeffs.shape[3]
+    share = split_count // 2
     legendre, fourier, weight, sine, cosine, lon = tables
     half = degrees // 2
     block = math.gcd(drops, 4)
+    steps = drops // block
     f32 = jnp.asarray(fourier, F32)
     coarse = f32.astype(BF16)
     fine = (f32 - coarse.astype(F32)).astype(BF16)
@@ -161,136 +291,85 @@
     folded = np.concatenate([weight[:half], weight[:half]]) / (8.0 * math.pi)
     weight_grid = jnp.asarray(np.broadcast_to(folded[:, None], (degrees, width)), F32)
     parity = [jnp.asarray(t) for t in parity_tables(legendre, weight)]
-    whole = lambda a: pl.BlockSpec(a.shape, lambda i: (0,) * a.ndim)
     smem = pl.BlockSpec(memory_space=pltpu.SMEM)
+    vmem = pl.BlockSpec(memory_space=pltpu.VMEM)
     consts = parity + [fourier_parts, project, weight_grid]
-    grid_spec = pl.BlockSpec((block, degrees, width), lambda i: (i, 0, 0))
+    at = lambda i: jnp.minimum(i, steps - 1)
+    grid_spec = pl.BlockSpec((block, degrees, width), lambda i: (at(i), 0, 0))
+    grid_shape = jax.ShapeDtypeStruct((drops, degrees, width), F32)
+    held = (share, fields, degrees, half_width)
     return pl.pallas_call(
         spectral_kernel,
-        grid=(drops // block,),
-        in_specs=[smem, smem, pl.BlockSpec((block, fields, degrees, width), lambda i: (i, 0, 0, 0))]
-        + [whole(a) for a in consts],
-        out_specs=[grid_spec] * 3,
-        out_shape=[jax.ShapeDtypeStruct((drops, degrees, width), F32)] * 3,
+        grid=(steps + 1,),
+        in_specs=[
+            smem, smem, smem,
+            pl.BlockSpec((block, fields, degrees, width), lambda i: (at(i), 0, 0, 0)),
+            pl.BlockSpec(memory_space=pl.ANY), vmem, vmem,
+        ]
+        + [vmem] * len(consts),
+        out_specs=[grid_spec] * 3 + [vmem, vmem],
+        out_shape=[grid_shape] * 3
+        + [
+            jax.ShapeDtypeStruct((share, degrees, width), F32),
+            jax.ShapeDtypeStruct((devices, drops, LANES), BF16),
+        ],
         scratch_shapes=[
             pltpu.VMEM((block, 3, degrees, width), F32),
             pltpu.VMEM((block, 6, half, width), F32),
             pltpu.VMEM((block * 3 * degrees, 2 * width), BF16),
             pltpu.VMEM((block, 2, half, width), F32),
-        ],
-        compiler_params=pltpu.CompilerParams(vmem_limit_bytes=32 << 20),
-        cost_estimate=pl.CostEstimate(
-            flops=drops * 5_000_000, bytes_accessed=drops * 300_000, transcendentals=drops * 8192
-        ),
-    )(degree, material.reshape(-1), coeffs, *consts)
-
-
-def place(index):
-    col_count = lax.axis_size("col")
-    return (index // col_count, index % col_count)
-
-
-def own_index():
-    return lax.axis_index("row") * lax.axis_size("col") + lax.axis_index("col")
-
-
-def greet(devices, me):
-    barrier = pltpu.get_barrier_semaphore()
-
-    def one(step, carry):
-        pl.semaphore_signal(
-            barrier, inc=1, device_id=place((me + step) % devices), device_id_type=MESH
-        )
-        return carry
-
-    lax.fori_loop(1, devices, one, 0)
-    return barrier
-
-
-def points_kernel(
-    degree_ref, coeffs_ref, basis_ref, out_ref, shape_scr, part_scr, send_scr, land_scr,
-    local_sem, send_sem, recv_sem,
-):
-    devices = out_ref.shape[0]
-    drops, fields, degrees, width = coeffs_ref.shape
-    point_count = basis_ref.shape[0]
-    me = own_index()
-    load = pltpu.make_async_copy(coeffs_ref.at[:, 0], shape_scr, local_sem)
-    load.start()
-    barrier = greet(devices, me)
-    load.wait()
-    level = lax.broadcasted_iota(jnp.int32, (degrees, width), 0)
-    for d in range(drops):
-        shape = jnp.where(level <= degree_ref[d], shape_scr[d], 0.0)
-        for p in range(point_count):
-            part_scr[p, d : d + 1, :] = jnp.sum(shape * basis_ref[p], axis=0, keepdims=True)
-    lane = lax.broadcasted_iota(jnp.int32, (drops, LANES), 1)
-    surface = jnp.zeros((drops, LANES), F32)
-    for p in range(point_count):
-        surface = jnp.where(lane == p, jnp.sum(part_scr[p], axis=1, keepdims=True), surface)
-    send_scr[...] = jnp.exp(surface).astype(BF16)
-    pl.semaphore_wait(barrier, devices - 1)
-
-    def copy(step):
-        return pltpu.make_async_remote_copy(
-            src_ref=send_scr,
-            dst_ref=land_scr.at[me],
-            send_sem=send_sem.at[step],
-            recv_sem=recv_sem.at[step],
-            device_id=place((me + step) % devices),
-            device_id_type=MESH,
-        )
-
-    def begin(step, carry):
-        copy(step).start()
-        return carry
-
-    def finish(step, carry):
-        copy(step).wait()
-        return carry
-
-    lax.fori_loop(1, devices, begin, 0)
-    land_scr[me] = send_scr[...]
-    lax.fori_loop(1, devices, finish, 0)
-    out_ref[...] = land_scr[...]
-
-
-def gather_points(degree, coeffs, basis, devices):
-    drops, fields, degrees, width = coeffs.shape
-    point_count = basis.shape[0]
-    vmem = pl.BlockSpec(memory_space=pltpu.VMEM)
-    return pl.pallas_call(
-        points_kernel,
-        in_specs=[
-            pl.BlockSpec(memory_space=pltpu.SMEM), pl.BlockSpec(memory_space=pl.ANY), vmem
-        ],
-        out_specs=vmem,
-        out_shape=jax.ShapeDtypeStruct((devices, drops, LANES), BF16),
-        scratch_shapes=[
             pltpu.VMEM((drops, degrees, width), F32),
-            pltpu.VMEM((point_count, drops, width), F32),
+            pltpu.VMEM((basis.shape[0], drops, width), F32),
             pltpu.VMEM((drops, LANES), BF16),
             pltpu.VMEM((devices, drops, LANES), BF16),
+            pltpu.VMEM(held, BF16),
+            pltpu.VMEM(held, BF16),
+            pltpu.VMEM((share, fields, degrees, width), F32),
             pltpu.SemaphoreType.DMA,
             pltpu.SemaphoreType.DMA((devices,)),
             pltpu.SemaphoreType.DMA((devices,)),
+            pltpu.SemaphoreType.DMA,
+            pltpu.SemaphoreType.DMA,
         ],
         compiler_params=pltpu.CompilerParams(
-            collective_id=0, has_side_effects=True, vmem_limit_bytes=32 << 20
+            collective_id=0, has_side_effects=True, vmem_limit_bytes=40 << 20
         ),
-    )(degree, coeffs, basis)
+    )(
+        degree, material.T, split_material.T, coeffs, coeffs, split_coeffs, basis, *consts
+    )
 
 
 def near_kernel(
-    normals, entry_ref, points_ref, radius_ref, load_ref, turn_ref, tilt_ref, out_ref,
-    target_scr, spread_scr, total_scr, send_scr, land_scr, send_sem, recv_sem,
+    normals, dev_ref, slot_ref, sep_ref, points_ref, radius_ref, load_ref, split_ref,
+    turn_ref, tilt_ref, out_ref, split_out_ref,
+    entry_ref, target_scr, spread_scr, total_scr, send_scr, land_scr, give_scr, came_scr,
+    send_sem, recv_sem, give_sem, came_sem,
 ):
     drops, degrees, width = radius_ref.shape
     devices = land_scr.shape[0]
     me = own_index()
-    barrier = greet(devices, me)
-    entries = entry_ref.shape[0]
-    readers = entries // drops
+    barrier = greet()
+    readers = dev_ref.shape[0]
+    entries = drops * readers
+    entry_lane = lax.broadcasted_iota(jnp.int32, (readers, LANES), 1)
+    for d in range(drops):
+        columns_of = [sep_ref[c, :, d : d + 1] for c in range(3)]
+        columns_of += [ref[:, d : d + 1].astype(F32) for ref in (dev_ref, slot_ref)]
+        rows_of = jnp.zeros((readers, LANES), F32)
+        for n, column in enumerate(columns_of):
+            rows_of = jnp.where(entry_lane == n, column, rows_of)
+        entry_ref[d * readers : (d + 1) * readers, :] = rows_of
+    share, split_width = split_ref.shape[0], split_ref.shape[2]
+    orders = split_width // 4
+    parity = lax.axis_index("row") % 2
+    for n in range(share):
+        whole = split_ref[n]
+        cut = [whole[:, k * orders : (k + 1) * orders] for k in range(4)]
+        lower = jnp.concatenate([cut[0], cut[2]], axis=1)
+        upper = jnp.concatenate([cut[1], cut[3]], axis=1)
+        give_scr[n] = jnp.where(parity == 0, upper, lower).astype(BF16)
+        split_out_ref[parity * share + n] = jnp.where(parity == 0, lower, upper)
+    swap = to_partner(give_scr, came_scr, give_sem, came_sem)
     half = degrees // 2
     targets = points_ref.shape[0]
     columns = spread_scr.shape[1]
@@ -367,7 +446,10 @@
         )
         return carry
 
-    lax.fori_loop(0, drops, one_drop, 0)
+    lax.fori_loop(0, drops // 2, one_drop, 0)
+    pl.semaphore_wait(barrier, devices - 1)
+    swap.start()
+    lax.fori_loop(drops // 2, drops, one_drop, 0)
     goes = lax.broadcasted_iota(jnp.int32, (entries, devices), 1) == to
     goes = goes.astype(F32).astype(BF16)
     spread = spread_scr[...]
@@ -378,61 +460,56 @@
         goes, coarse, first, preferred_element_type=F32
     ) + lax.dot_general(goes, fine, first, preferred_element_type=F32)
 
-    def lay(device, carry):
-        send_scr[device] = total_scr[pl.ds(device, 1), :]
-        return carry
-
-    lax.fori_loop(0, devices, lay, 0)
-    pl.semaphore_wait(barrier, devices - 1)
-
-    def copy(step):
-        other = (me + step) % devices
-        return pltpu.make_async_remote_copy(
-            src_ref=send_scr.at[other],
-            dst_ref=land_scr.at[me],
-            send_sem=send_sem.at[step],
-            recv_sem=recv_sem.at[step],
-            device_id=place(other),
-            device_id_type=MESH,
-        )
-
-    def begin(step, carry):
-        copy(step).start()
-        return carry
-
-    def finish(step, carry):
-        copy(step).wait()
-        return carry
-
-    lax.fori_loop(1, devices, begin, 0)
+    for device in range(devices):
+        send_scr[device] = total_scr[device : device + 1, :]
+    col_count = lax.axis_size("col")
+    copies = to_all(
+        lambda peer: send_scr.at[peer[0] * col_count + peer[1]], land_scr, send_sem, recv_sem
+    )
+    for copy in copies:
+        copy.start()
     land_scr[me] = send_scr[me]
-    lax.fori_loop(1, devices, finish, 0)
+    swap.wait()
+    split_out_ref[pl.ds((1 - parity) * share, share)] = came_scr[...].astype(F32)
+    for copy in copies:
+        copy.wait()
     velocity = jnp.sum(land_scr[...], axis=0)
     for c in range(3):
         out_ref[c : c + 1, :] = velocity[:, c * block : (c + 1) * block]
 
 
-def near(entry, points, radius, load, tables, normals, devices, columns):
+def near(dev, slot, sep, points, radius, load, split_out, tables, normals, devices, columns):
     legendre, fourier, weight, sine, cosine, lon = tables
     drops, degrees, width = radius.shape
+    share = split_out.shape[0]
     half = degrees // 2
     turn = jnp.asarray(np.stack([np.cos(lon), np.sin(lon)]), F32)
     tilt = np.stack([sine[:half], cosine[:half]])
     tilt = jnp.asarray(np.broadcast_to(tilt[:, :, None], (2, half, width)), F32)
-    entries = entry.shape[0]
+    entries = drops * dev.shape[0]
+    vmem = pl.BlockSpec(memory_space=pltpu.VMEM)
+    held = (share, degrees, width // 2)
     return pl.pallas_call(
         functools.partial(near_kernel, normals),
-        in_specs=[pl.BlockSpec(memory_space=pltpu.VMEM)] * 6,
-        out_specs=pl.BlockSpec(memory_space=pltpu.VMEM),
-        out_shape=jax.ShapeDtypeStruct((3, drops * len(normals)), F32),
+        in_specs=[vmem] * 9,
+        out_specs=[vmem, vmem],
+        out_shape=[
+            jax.ShapeDtypeStruct((3, drops * len(normals)), F32),
+            jax.ShapeDtypeStruct((2 * share, degrees, width // 2), F32),
+        ],
         scratch_shapes=[
+            pltpu.VMEM((entries, LANES), F32),
             pltpu.VMEM((entries, LANES), F32),
             pltpu.VMEM((entries, columns), F32),
             pltpu.VMEM((devices, columns), F32),
             pltpu.VMEM((devices, 1, columns), F32),
             pltpu.VMEM((devices, 1, columns), F32),
+            pltpu.VMEM(held, BF16),
+            pltpu.VMEM(held, BF16),
             pltpu.SemaphoreType.DMA((devices,)),
             pltpu.SemaphoreType.DMA((devices,)),
+            pltpu.SemaphoreType.DMA,
+            pltpu.SemaphoreType.DMA,
         ],
         compiler_params=pltpu.CompilerParams(
             collective_id=1, has_side_effects=True, vmem_limit_bytes=32 << 20
@@ -440,15 +517,13 @@
         cost_estimate=pl.CostEstimate(
             flops=entries * 4 * 8192 * 20, bytes_accessed=2_000_000, transcendentals=entries * 32768
         ),
-    )(entry, points, radius, load, turn, tilt)
+    )(dev, slot, sep, points, radius, load, split_out, turn, tilt)
 
 
 def per_device(
     coeffs, degree, material, split_coeffs, split_material, separation, reader_dev, reader_slot
 ):
     drops, fields, degrees, width = coeffs.shape
-    readers = reader_dev.shape[1]
-    entries = drops * readers
     row_count, col_count = lax.axis_size("row"), lax.axis_size("col")
     devices = row_count * col_count
     tables = spectral_tables(degrees)
@@ -470,49 +545,15 @@
     basis = jnp.asarray(
         np.stack([legendre[order, j, :].T * fourier[:, k][None, :] for j, k in spots]), F32
     )
-    all_points = gather_points(degree, coeffs, basis, devices)
-
-    split_count = split_coeffs.shape[0]
-    share = split_count // 2
-    half_orders = split_coeffs.shape[3] // 2
-    row, col = lax.axis_index("row"), lax.axis_index("col")
-    parity = row % 2
-    route = [(r, r ^ 1) for r in range(row_count)]
-    mine = lax.dynamic_slice_in_dim(split_coeffs, parity * share, share, 0)
-    theirs = lax.dynamic_slice_in_dim(split_coeffs, (1 - parity) * share, share, 0)
-    came = lax.ppermute(theirs.astype(BF16), "row", route).astype(F32)
-
-    traction_coeffs, radius, load = spectral(coeffs, degree, material, tables)
-
-    wide = (share, fields, degrees, 2, half_orders)
-    mine, came = mine.reshape(wide), came.reshape(wide)
-    lower = jnp.where(parity == 0, mine, came)
-    upper = jnp.where(parity == 0, came, mine)
-    full = jnp.stack([lower, upper], axis=4).reshape(share, fields, degrees, width)
-    pair_start = (row // 2 * col_count + col) * split_count + parity * share
-    own_material = lax.dynamic_slice_in_dim(split_material, pair_start, share, 0)
-    top = jnp.full((share,), degrees - 1, jnp.int32)
-    split_out, _, _ = spectral(full, top, own_material, tables)
-    cut = split_out.reshape(share, degrees, 2, 2, half_orders)
-    kept = jnp.where(parity == 0, cut[:, :, :, 0], cut[:, :, :, 1])
-    given = jnp.where(parity == 0, cut[:, :, :, 1], cut[:, :, :, 0]).astype(BF16)
-    kept = kept.reshape(share, degrees, 2 * half_orders)
-    got = lax.ppermute(given.reshape(kept.shape), "row", route).astype(F32)
-
+    traction_coeffs, radius, load, split_out, points = spectral(
+        coeffs, degree, material, split_coeffs, split_material, basis, tables, devices
+    )
     point_count = len(spots)
     columns = -(-3 * drops * point_count // LANES) * LANES
-    entry = jnp.concatenate(
-        [
-            jnp.transpose(separation, (1, 2, 0)),
-            reader_dev.astype(F32)[:, :, None],
-            reader_slot.astype(F32)[:, :, None],
-        ],
-        axis=2,
-    ).reshape(entries, 5)
-    table = all_points.reshape(devices * drops, LANES)
-    velocity = near(entry, table, radius, load, tables, normals, devices, columns)
-    split_traction = jnp.where(
-        parity == 0, jnp.concatenate([kept, got]), jnp.concatenate([got, kept])
+    velocity, split_traction = near(
+        reader_dev.T, reader_slot.T, jnp.transpose(separation, (0, 2, 1)),
+        points.reshape(devices * drops, LANES), radius, load, split_out,
+        tables, normals, devices, columns,
     )
     return traction_coeffs, split_traction, velocity
 

time: 68.2 us -> 55.1 us (0.81)
  Pallas kernels: 47.3 us -> 39.8 us
  starting transfers between devices: 3.81 us -> 0 us
  waiting for transfers between devices: 3.25 us -> 0 us
  local copies, waits for them, and re-layouts: 11 us -> 13.9 us
  other arithmetic: 1.49 us -> 0 us
    pallas_call x4 -> x2, Pallas kernels: 47.3 us -> 39.8 us  [the longest x1 22.2 us: near(): pl.pallas_call(functools.partial(near_kernel, normals), in_specs=[vmem] *...]
    unnamed x37 -> x39, local copies, waits for them, and re-layouts: 8.38 us -> 13.9 us
    ppermute x2 -> x0, starting transfers between devices: 3.81 us -> none  [the longest x1 3.09 us: per_device(): came = lax.ppermute(theirs.astype(BF16), 'row', route).astype(F32)]
    ppermute x2 -> x0, waiting for transfers between devices: 3.25 us -> none  [the longest x1 3.25 us: per_device(): got = lax.ppermute(given.reshape(kept.shape), 'row', route).astype(F32)]
    convert_element_type x4 -> x0, other arithmetic: 1.4 us -> none  [the longest x1 0.69 us: per_device(): reader_slot.astype(F32)[:, :, None]]
    dynamic_slice x4 -> x0, local copies, waits for them, and re-layouts: 0.89 us -> none  [the longest x2 0.85 us: per_device(): lax.dynamic_slice_in_dim(split_material, pair_start, share, 0)]
    transpose x1 -> x0, local copies, waits for them, and re-layouts: 0.78 us -> none  [per_device(): jnp.transpose(separation, (1, 2, 0))]
  transfers between devices with their start and end apart: 2 -> 0, of which waited for: 1 -> 0; matrix products, arithmetic and copies ran while one was open for 7% -> 0% of each run, Pallas kernels for 67% -> 0%
where the time goes in v3:
time: 55.1 us; the launch traced here: 54.5 us
  Pallas kernels  39.8 us (72%)
  local copies, waits for them, and re-layouts  13.9 us (25%)
  between operations  0.72 us (1%)
    pallas_call x1, Pallas kernels, near(): pl.pallas_call(functools.partial(near_kernel, normals), in_specs=[vmem] *...  22.2 us
    pallas_call x1, Pallas kernels, spectral(): pl.pallas_call(spectral_kernel, grid=(steps + 1,), in_specs=[smem, smem,...  17.6 us
    unnamed x39, local copies, waits for them, and re-layouts  13.9 us

profile of v3, /device:TPU:0, one launch (start us, length us, event | category | flops | bytes accessed | tf_op | source)
XLA Modules:
  0.0 54.5 jit_solution(3149241562612926022)
XLA Ops:
  0.6 0.0 copy-start
  0.6 1.4 %copy-done = f32[16,3,64,128]{3,2,1,0:T(8,128)S(1)} copy-done((f32[16,3,64,128]{3,2,1,0:T(8,128)S(1)}, f32[16,3,64,128]{3,2,1,0:T(8,128)}, u32[]{:S(2)}) %copy-start) | copy-done | bytes 1572888
  2.0 0.0 copy-start.1
  2.0 1.0 %copy-done.1 = f32[32,32,128]{2,1,0:T(8,128)S(1)} copy-done((f32[32,32,128]{2,1,0:T(8,128)S(1)}, f32[32,32,128]{2,1,0:T(8,128)}, u32[]{:S(2)}) %copy-start.1) | copy-done | bytes 524312
  3.1 0.0 copy-start.2
  3.1 1.0 %copy-done.2 = f32[32,32,128]{2,1,0:T(8,128)S(1)} copy-done((f32[32,32,128]{2,1,0:T(8,128)S(1)}, f32[32,32,128]{2,1,0:T(8,128)}, u32[]{:S(2)}) %copy-start.2) | copy-done | bytes 524312
  4.1 0.0 copy-start.3
  4.1 1.0 %copy-done.3 = f32[32,32,128]{2,1,0:T(8,128)S(1)} copy-done((f32[32,32,128]{2,1,0:T(8,128)S(1)}, f32[32,32,128]{2,1,0:T(8,128)}, u32[]{:S(2)}) %copy-start.3) | copy-done | bytes 524312
  5.2 0.0 copy-start.4
  5.2 1.0 %copy-done.4 = f32[32,32,128]{2,1,0:T(8,128)S(1)} copy-done((f32[32,32,128]{2,1,0:T(8,128)S(1)}, f32[32,32,128]{2,1,0:T(8,128)}, u32[]{:S(2)}) %copy-start.4) | copy-done | bytes 524312
  6.2 0.0 copy-start.5
  6.2 1.0 %copy-done.5 = f32[4,3,64,64]{3,2,1,0:T(8,128)S(1)} copy-done((f32[4,3,64,64]{3,2,1,0:T(8,128)S(1)}, f32[4,3,64,64]{3,2,1,0:T(8,128)}, u32[]{:S(2)}) %copy-start.5) | copy-done | bytes 196632
  7.2 0.0 copy-start.6
  7.2 0.9 %copy-done.6 = f32[4,64,128]{2,1,0:T(8,128)S(1)} copy-done((f32[4,64,128]{2,1,0:T(8,128)S(1)}, f32[4,64,128]{2,1,0:T(8,128)}, u32[]{:S(2)}) %copy-start.6) | copy-done | bytes 131096
  8.1 0.0 copy-start.7
  8.1 0.9 %copy-done.7 = bf16[256,256]{1,0:T(8,128)(2,1)S(1)} copy-done((bf16[256,256]{1,0:T(8,128)(2,1)S(1)}, bf16[256,256]{1,0:T(8,128)(2,1)}, u32[]{:S(2)}) %copy-start.7) | copy-done | bytes 131096
  9.0 0.0 copy-start.8
  9.0 0.8 %copy-done.8 = bf16[128,128]{1,0:T(8,128)(2,1)S(1)} copy-done((bf16[128,128]{1,0:T(8,128)(2,1)S(1)}, bf16[128,128]{1,0:T(8,128)(2,1)}, u32[]{:S(2)}) %copy-start.8) | copy-done | bytes 32792
  9.8 0.0 copy-start.9
  9.8 0.8 %copy-done.9 = f32[64,128]{1,0:T(8,128)S(1)} copy-done((f32[64,128]{1,0:T(8,128)S(1)}, f32[64,128]{1,0:T(8,128)}, u32[]{:S(2)}) %copy-start.9) | copy-done | bytes 32792
  10.5 0.0 copy-start.10
  10.5 0.7 %copy-done.10 = f32[16,2]{0,1:T(2,128)S(1)} copy-done((f32[16,2]{0,1:T(2,128)S(1)}, f32[16,2]{0,1:T(2,128)}, u32[]{:S(2)}) %copy-start.10) | copy-done | bytes 152
  11.2 0.0 copy-start.11
  11.2 0.7 %copy-done.11 = f32[64,2]{0,1:T(2,128)S(1)} copy-done((f32[64,2]{0,1:T(2,128)S(1)}, f32[64,2]{0,1:T(2,128)}, u32[]{:S(2)}) %copy-start.11) | copy-done | bytes 536
  11.9 0.0 copy-start.12
  11.9 0.7 %copy-done.12 = s32[16]{0:T(128)S(1)} copy-done((s32[16]{0:T(128)S(1)}, s32[16]{0:T(128)}, u32[]{:S(2)}) %copy-start.12) | copy-done | bytes 88
  12.5 0.0 copy-start.13
  12.6 0.0 copy-start.14
  12.6 0.0 copy-start.15
  12.6 0.0 copy-start.16
  12.6 0.0 copy-start.17
  12.6 17.6 %shard_map.193 = (f32[16,64,128]{2,1,0:T(8,128)S(1)}, f32[16,64,128]{2,1,0:T(8,128)S(1)}, f32[16,64,128]{2,1,0:T(8,128)S(1)}, f32[2,64,128]{2,1,0:T(8,128)S(1)}, bf16[32,16,128]{2,1,0:T(8,128)(2,1)S(1)}) custom-call(s32[16]{0:T(128)S(1)} %copy-done.12, f32[2,16]{1,0:T(2,128)S(1)} %bitcast.6, f32[2,64]{1,0:T(2,128)S(1)} %bitcast.7, ...), custom_call_target="tpu_custom_call" | custom-call | tf_op jit(solution)/shard_map/pallas_call | solution.py:301
  30.2 0.0 copy-done.13
  30.2 0.0 copy-done.14
  30.2 0.0 copy-done.15
  30.2 0.0 copy-done.16
  30.2 0.0 copy-done.17
  30.2 22.2 %shard_map.194 = (f32[3,64]{1,0:T(4,128)S(1)}, f32[4,64,64]{2,1,0:T(8,128)S(1)}) custom-call(s32[8,16]{1,0:T(8,128)S(1)} %bitcast.10, s32[8,16]{1,0:T(8,128)S(1)} %bitcast.11, f32[3,8,16]{2,1,0:T(8,128)S(1)} %bitcast.9, bf16[512,128]{1,0:T(8,128)(2,1)S(1)} %bitcast.8, f32[16,64,128]{2,1,0:T(8,128)S(1)} %get-tuple-element.12.radius_ref, ...), custom_call_target="tpu_custom_call" | custom-call | flops 83886080 | bytes 2000000 | tf_op jit(solution)/shard_map/pallas_call | solution.py:492
  52.5 0.8 %copy.24 = f32[16,64,128]{2,1,0:T(8,128)} copy(f32[16,64,128]{2,1,0:T(8,128)S(1)} %get-tuple-element.20) | data formatting | bytes 1048576
  53.3 0.7 %copy.25 = f32[4,64,64]{2,1,0:T(8,128)} copy(f32[4,64,64]{2,1,0:T(8,128)S(1)} %get-tuple-element.21) | data formatting | bytes 131072
  53.9 0.6 %copy.26 = f32[3,64]{1,0:T(4,128)} copy(f32[3,64]{1,0:T(4,128)S(1)} %get-tuple-element.22) | data formatting | bytes 1536
Async XLA Ops:
  0.6 1.4 %copy-start = (f32[16,3,64,128]{3,2,1,0:T(8,128)S(1)}, f32[16,3,64,128]{3,2,1,0:T(8,128)}, u32[]{:S(2)}) copy-start(f32[16,3,64,128]{3,2,1,0:T(8,128)} %all_coeffs_ref.1) | copy-start | bytes 4718596
  2.0 1.0 %copy-start.1 = (f32[32,32,128]{2,1,0:T(8,128)S(1)}, f32[32,32,128]{2,1,0:T(8,128)}, u32[]{:S(2)}) copy-start(f32[32,32,128]{2,1,0:T(8,128)} %constant.26.clone.rest_0_) | copy-start | bytes 1572868
  3.1 1.0 %copy-start.2 = (f32[32,32,128]{2,1,0:T(8,128)S(1)}, f32[32,32,128]{2,1,0:T(8,128)}, u32[]{:S(2)}) copy-start(f32[32,32,128]{2,1,0:T(8,128)} %constant.27.clone.rest_1_) | copy-start | bytes 1572868
  4.1 1.0 %copy-start.3 = (f32[32,32,128]{2,1,0:T(8,128)S(1)}, f32[32,32,128]{2,1,0:T(8,128)}, u32[]{:S(2)}) copy-start(f32[32,32,128]{2,1,0:T(8,128)} %constant.28.clone.rest_2_) | copy-start | bytes 1572868
  5.2 1.0 %copy-start.4 = (f32[32,32,128]{2,1,0:T(8,128)S(1)}, f32[32,32,128]{2,1,0:T(8,128)}, u32[]{:S(2)}) copy-start(f32[32,32,128]{2,1,0:T(8,128)} %constant.29.clone.rest_3_) | copy-start | bytes 1572868
  6.2 1.0 %copy-start.5 = (f32[4,3,64,64]{3,2,1,0:T(8,128)S(1)}, f32[4,3,64,64]{3,2,1,0:T(8,128)}, u32[]{:S(2)}) copy-start(f32[4,3,64,64]{3,2,1,0:T(8,128)} %split_ref.1) | copy-start | bytes 589828
  7.2 0.9 %copy-start.6 = (f32[4,64,128]{2,1,0:T(8,128)S(1)}, f32[4,64,128]{2,1,0:T(8,128)}, u32[]{:S(2)}) copy-start(f32[4,64,128]{2,1,0:T(8,128)} %constant.22.clone.basis_ref) | copy-start | bytes 393220
  8.1 0.9 %copy-start.7 = (bf16[256,256]{1,0:T(8,128)(2,1)S(1)}, bf16[256,256]{1,0:T(8,128)(2,1)}, u32[]{:S(2)}) copy-start(bf16[256,256]{1,0:T(8,128)(2,1)} %constant.47.rest_4_) | copy-start | bytes 393220
  9.0 0.8 %copy-start.8 = (bf16[128,128]{1,0:T(8,128)(2,1)S(1)}, bf16[128,128]{1,0:T(8,128)(2,1)}, u32[]{:S(2)}) copy-start(bf16[128,128]{1,0:T(8,128)(2,1)} %constant.24.clone.rest_5_) | copy-start | bytes 98308
  9.8 0.8 %copy-start.9 = (f32[64,128]{1,0:T(8,128)S(1)}, f32[64,128]{1,0:T(8,128)}, u32[]{:S(2)}) copy-start(f32[64,128]{1,0:T(8,128)} %constant.25.clone.rest_6_) | copy-start | bytes 98308
  10.5 0.7 %copy-start.10 = (f32[16,2]{0,1:T(2,128)S(1)}, f32[16,2]{0,1:T(2,128)}, u32[]{:S(2)}) copy-start(f32[16,2]{0,1:T(2,128)} %param.20) | copy-start | bytes 388
  11.2 0.7 %copy-start.11 = (f32[64,2]{0,1:T(2,128)S(1)}, f32[64,2]{0,1:T(2,128)}, u32[]{:S(2)}) copy-start(f32[64,2]{0,1:T(2,128)} %param.22) | copy-start | bytes 1540
  11.9 0.7 %copy-start.12 = (s32[16]{0:T(128)S(1)}, s32[16]{0:T(128)}, u32[]{:S(2)}) copy-start(s32[16]{0:T(128)} %degree_ref.1) | copy-start | bytes 196
  12.5 17.7 %copy-start.13 = (f32[3,16,8]{1,2,0:T(8,128)S(1)}, f32[3,16,8]{1,2,0:T(8,128)}, u32[]{:S(2)}) copy-start(f32[3,16,8]{1,2,0:T(8,128)} %param.23) | copy-start | bytes 4612
  12.6 17.7 %copy-start.14 = (s32[16,8]{0,1:T(8,128)S(1)}, s32[16,8]{0,1:T(8,128)}, u32[]{:S(2)}) copy-start(s32[16,8]{0,1:T(8,128)} %param.24) | copy-start | bytes 1540
  12.6 17.7 %copy-start.15 = (s32[16,8]{0,1:T(8,128)S(1)}, s32[16,8]{0,1:T(8,128)}, u32[]{:S(2)}) copy-start(s32[16,8]{0,1:T(8,128)} %param.25) | copy-start | bytes 1540
  12.6 17.7 %copy-start.16 = (f32[2,32,128]{2,1,0:T(8,128)S(1)}, f32[2,32,128]{2,1,0:T(8,128)}, u32[]{:S(2)}) copy-start(f32[2,32,128]{2,1,0:T(8,128)} %constant.31.clone.tilt_ref) | copy-start | bytes 98308
  12.6 17.7 %copy-start.17 = (f32[2,128]{1,0:T(2,128)S(1)}, f32[2,128]{1,0:T(2,128)}, u32[]{:S(2)}) copy-start(f32[2,128]{1,0:T(2,128)} %constant.30.clone.turn_ref) | copy-start | bytes 3076

commit v4 on v3

--- a/solution.py
+++ b/solution.py
@@ -3,6 +3,7 @@
 
 import jax
 import jax.numpy as jnp
+import ml_dtypes
 import numpy as np
 from jax import lax
 from jax.experimental import pallas as pl
@@ -10,6 +11,7 @@
 from jax.sharding import PartitionSpec as P
 
 SOFTENING = 0.04
+VMEM_BYTES = 60 << 20
 LANES = 128
 F32 = jnp.float32
 BF16 = jnp.bfloat16
@@ -278,16 +280,11 @@
     half = degrees // 2
     block = math.gcd(drops, 4)
     steps = drops // block
-    f32 = jnp.asarray(fourier, F32)
-    coarse = f32.astype(BF16)
-    fine = (f32 - coarse.astype(F32)).astype(BF16)
-    fourier_parts = jnp.concatenate(
-        [
-            jnp.concatenate([coarse, fine], axis=1),
-            jnp.concatenate([coarse, jnp.zeros_like(fine)], axis=1),
-        ]
-    )
-    project = jnp.asarray(fourier.T, BF16)
+    exact = np.asarray(fourier, np.float32)
+    coarse = exact.astype(ml_dtypes.bfloat16)
+    fine = (exact - coarse.astype(np.float32)).astype(ml_dtypes.bfloat16)
+    fourier_parts = jnp.asarray(np.block([[coarse, fine], [coarse, np.zeros_like(fine)]]))
+    project = jnp.asarray(np.ascontiguousarray(coarse.T))
     folded = np.concatenate([weight[:half], weight[:half]]) / (8.0 * math.pi)
     weight_grid = jnp.asarray(np.broadcast_to(folded[:, None], (degrees, width)), F32)
     parity = [jnp.asarray(t) for t in parity_tables(legendre, weight)]
@@ -332,7 +329,7 @@
             pltpu.SemaphoreType.DMA,
         ],
         compiler_params=pltpu.CompilerParams(
-            collective_id=0, has_side_effects=True, vmem_limit_bytes=40 << 20
+            collective_id=0, has_side_effects=True, vmem_limit_bytes=VMEM_BYTES
         ),
     )(
         degree, material.T, split_material.T, coeffs, coeffs, split_coeffs, basis, *consts
@@ -410,7 +407,7 @@
             g = (inv * h) * (inv * inv)
             return g * ((rho - m) + SOFTENING), g * off
 
-        def tile(jt, acc):
+        def tile(points, jt, acc):
             acc = list(acc)
             base = pl.multiple_of(jt * 8, 8)
             for q in range(8):
@@ -422,18 +419,23 @@
                 s = tilt_ref[0, pl.ds(j, 1), :]
                 c = tilt_ref[1, pl.ds(j, 1), :]
                 q0, q1 = r0 * r0, r1 * r1
-                for p in range(point_count):
+                for n, p in enumerate(points):
                     flat = s * ring[p]
                     up = c * height[p]
                     w0, v0 = cell(flat + up, r0, q0, h0, square[p])
                     w1, v1 = cell(flat - up, r1, q1, h1, square[p])
-                    acc[3 * p] = acc[3 * p] + s * (w0 + w1)
-                    acc[3 * p + 1] = acc[3 * p + 1] + c * (w0 - w1)
-                    acc[3 * p + 2] = acc[3 * p + 2] + (v0 + v1)
+                    acc[3 * n] = acc[3 * n] + s * (w0 + w1)
+                    acc[3 * n + 1] = acc[3 * n + 1] + c * (w0 - w1)
+                    acc[3 * n + 2] = acc[3 * n + 2] + (v0 + v1)
             return tuple(acc)
 
         zero = jnp.zeros((readers, width), F32)
-        acc = lax.fori_loop(0, half // 8, tile, (zero,) * (3 * point_count))
+        acc = ()
+        for low in range(0, point_count, 2):
+            points = range(low, min(low + 2, point_count))
+            acc += lax.fori_loop(
+                0, half // 8, functools.partial(tile, points), (zero,) * (3 * len(points))
+            )
         spread = jnp.zeros((readers, columns), F32)
         for p in range(point_count):
             around, up, along = acc[3 * p : 3 * p + 3]
@@ -512,7 +514,7 @@
             pltpu.SemaphoreType.DMA,
         ],
         compiler_params=pltpu.CompilerParams(
-            collective_id=1, has_side_effects=True, vmem_limit_bytes=32 << 20
+            collective_id=1, has_side_effects=True, vmem_limit_bytes=VMEM_BYTES
         ),
         cost_estimate=pl.CostEstimate(
             flops=entries * 4 * 8192 * 20, bytes_accessed=2_000_000, transcendentals=entries * 32768

time: 55.1 us -> 48.2 us (0.87)
  local copies, waits for them, and re-layouts: 13.9 us -> 3.62 us
  Pallas kernels: 39.8 us -> 43.7 us
    unnamed x39 -> x5, local copies, waits for them, and re-layouts: 13.9 us -> 3.62 us
    pallas_call x1, Pallas kernels: 22.2 us -> 24.6 us  [near(): pl.pallas_call(functools.partial(near_kernel, normals), in_specs=[vmem] *...]
    pallas_call x1, Pallas kernels: 17.6 us -> 19.1 us  [spectral(): pl.pallas_call(spectral_kernel, grid=(steps + 1,), in_specs=[smem, smem,...]
where the time goes in v4:
time: 48.2 us; the launch traced here: 48 us
  Pallas kernels  43.7 us (91%)
  local copies, waits for them, and re-layouts  3.62 us (8%)
  between operations  0.66 us (1%)
    pallas_call x1, Pallas kernels, near(): pl.pallas_call(functools.partial(near_kernel, normals), in_specs=[vmem] *...  24.6 us
    pallas_call x1, Pallas kernels, spectral(): pl.pallas_call(spectral_kernel, grid=(steps + 1,), in_specs=[smem, smem,...  19.1 us
    unnamed x5, local copies, waits for them, and re-layouts  3.62 us

profile of v4, /device:TPU:0, one launch (start us, length us, event | category | flops | bytes accessed | tf_op | source)
XLA Modules:
  0.0 48.0 jit_solution(758387877118760456)
XLA Ops:
  0.6 19.1 %shard_map.193 = (f32[16,64,128]{2,1,0:T(8,128)}, f32[16,64,128]{2,1,0:T(8,128)}, f32[16,64,128]{2,1,0:T(8,128)}, f32[2,64,128]{2,1,0:T(8,128)}, bf16[32,16,128]{2,1,0:T(8,128)(2,1)}) custom-call(s32[16]{0:T(128)} %degree_ref.1, f32[2,16]{1,0:T(2,128)} %bitcast.6, f32[2,64]{1,0:T(2,128)} %bitcast.7, f32[16,3,64,128]{3,2,1,0:T(8,128)} %all_coeffs_ref.1, ...), custom_call_target="tpu_custom_call" | custom-call | tf_op jit(solution)/shard_map/pallas_call | solution.py:298
  19.7 0.0 copy-start
  19.7 24.6 %shard_map.194 = (f32[3,64]{1,0:T(4,128)}, f32[4,64,64]{2,1,0:T(8,128)}) custom-call(s32[8,16]{1,0:T(8,128)} %bitcast.10, s32[8,16]{1,0:T(8,128)} %bitcast.11, f32[3,8,16]{2,1,0:T(8,128)} %bitcast.9, bf16[512,128]{1,0:T(8,128)(2,1)} %bitcast.8, f32[16,64,128]{2,1,0:T(8,128)} %get-tuple-element.12.radius_ref, f32[16,64,128]{2,1,0:T(8,128)} %get-tuple-element.13.load_ref, ...), custom_call_target="tpu_custom_call" | custom-call | flops 83886080 | bytes 2000000 | tf_op jit(solution)/shard_map/pallas_call | solution.py:494
  44.4 0.0 copy-done
  44.4 0.8 %copy.24 = f32[16,64,128]{2,1,0:T(8,128)} copy(f32[16,64,128]{2,1,0:T(8,128)S(1)} %copy-done) | data formatting | bytes 1048576
  45.2 1.6 %copy.25 = f32[4,64,64]{2,1,0:T(8,128)} copy(f32[4,64,64]{2,1,0:T(8,128)} %get-tuple-element.21) | data formatting | bytes 131072
  46.7 1.2 %copy.26 = f32[3,64]{1,0:T(4,128)} copy(f32[3,64]{1,0:T(4,128)} %get-tuple-element.22) | data formatting | bytes 1536
Async XLA Ops:
  19.7 24.7 %copy-start = (f32[16,64,128]{2,1,0:T(8,128)S(1)}, f32[16,64,128]{2,1,0:T(8,128)}, u32[]{:S(2)}) copy-start(f32[16,64,128]{2,1,0:T(8,128)} %get-tuple-element.20) | copy-start | bytes 1572868

commit v5 on v4

--- a/solution.py
+++ b/solution.py
@@ -431,8 +431,8 @@
 
         zero = jnp.zeros((readers, width), F32)
         acc = ()
-        for low in range(0, point_count, 2):
-            points = range(low, min(low + 2, point_count))
+        for low in range(0, point_count, 4):
+            points = range(low, min(low + 4, point_count))
             acc += lax.fori_loop(
                 0, half // 8, functools.partial(tile, points), (zero,) * (3 * len(points))
             )

time: 48.2 us -> 47.3 us (0.981)
  Pallas kernels: 43.7 us -> 42.8 us
    pallas_call x1, Pallas kernels: 24.6 us -> 23.8 us  [near(): pl.pallas_call(functools.partial(near_kernel, normals), in_specs=[vmem] *...]
where the time goes in v5:
time: 47.3 us; the launch traced here: 47.1 us
  Pallas kernels  42.8 us (90%)
  local copies, waits for them, and re-layouts  3.62 us (8%)
  between operations  0.66 us (1%)
    pallas_call x1, Pallas kernels, near(): pl.pallas_call(functools.partial(near_kernel, normals), in_specs=[vmem] *...  23.8 us
    pallas_call x1, Pallas kernels, spectral(): pl.pallas_call(spectral_kernel, grid=(steps + 1,), in_specs=[smem, smem,...  19.1 us
    unnamed x5, local copies, waits for them, and re-layouts  3.62 us

profile of v5, /device:TPU:0, one launch (start us, length us, event | category | flops | bytes accessed | tf_op | source)
XLA Modules:
  0.0 47.1 jit_solution(11839599219613679153)
XLA Ops:
  0.6 19.1 %shard_map.193 = (f32[16,64,128]{2,1,0:T(8,128)}, f32[16,64,128]{2,1,0:T(8,128)}, f32[16,64,128]{2,1,0:T(8,128)}, f32[2,64,128]{2,1,0:T(8,128)}, bf16[32,16,128]{2,1,0:T(8,128)(2,1)}) custom-call(s32[16]{0:T(128)} %degree_ref.1, f32[2,16]{1,0:T(2,128)} %bitcast.6, f32[2,64]{1,0:T(2,128)} %bitcast.7, f32[16,3,64,128]{3,2,1,0:T(8,128)} %all_coeffs_ref.1, ...), custom_call_target="tpu_custom_call" | custom-call | tf_op jit(solution)/shard_map/pallas_call | solution.py:298
  19.7 0.0 copy-start
  19.7 23.8 %shard_map.194 = (f32[3,64]{1,0:T(4,128)}, f32[4,64,64]{2,1,0:T(8,128)}) custom-call(s32[8,16]{1,0:T(8,128)} %bitcast.10, s32[8,16]{1,0:T(8,128)} %bitcast.11, f32[3,8,16]{2,1,0:T(8,128)} %bitcast.9, bf16[512,128]{1,0:T(8,128)(2,1)} %bitcast.8, f32[16,64,128]{2,1,0:T(8,128)} %get-tuple-element.12.radius_ref, f32[16,64,128]{2,1,0:T(8,128)} %get-tuple-element.13.load_ref, ...), custom_call_target="tpu_custom_call" | custom-call | flops 83886080 | bytes 2000000 | tf_op jit(solution)/shard_map/pallas_call | solution.py:494
  43.5 0.0 copy-done
  43.5 0.8 %copy.24 = f32[16,64,128]{2,1,0:T(8,128)} copy(f32[16,64,128]{2,1,0:T(8,128)S(1)} %copy-done) | data formatting | bytes 1048576
  44.3 1.6 %copy.25 = f32[4,64,64]{2,1,0:T(8,128)} copy(f32[4,64,64]{2,1,0:T(8,128)} %get-tuple-element.21) | data formatting | bytes 131072
  45.8 1.2 %copy.26 = f32[3,64]{1,0:T(4,128)} copy(f32[3,64]{1,0:T(4,128)} %get-tuple-element.22) | data formatting | bytes 1536
Async XLA Ops:
  19.7 23.8 %copy-start = (f32[16,64,128]{2,1,0:T(8,128)S(1)}, f32[16,64,128]{2,1,0:T(8,128)}, u32[]{:S(2)}) copy-start(f32[16,64,128]{2,1,0:T(8,128)} %get-tuple-element.20) | copy-start | bytes 1572868
